TPU v7x, 128 devices: a whole 4x4x4 slice. The times are simulated.
128 devices in a mesh: band: 64 (over z, y, x), head: 2 (over core).
Axes of the slice: x: 4, y: 4, z: 4, core: 2. Of those that a mesh axis runs over, the one named last changes fastest.
Arguments:
- grid_in: bfloat16 [262144, 128], P('band'), may hold values from -6 to 6
- mesh_in: bfloat16 [16384, 1024], P('band'), may hold values from -6 to 6
- counts: int32 [64], replicated, may hold values from 1 to 256, 12288 in all
- enc_edges: int32 [12, 16384], P(None, 'band'), may hold values from 0 to 262143, as said below
- enc_bias: float32 [12, 16, 16384], P(None, 'head', 'band'), may hold values from -90 to 160
- proc_bias: float32 [257, 16, 16384], P(None, 'head', 'band'), may hold values from -90 to 160
- w_embed: bfloat16 [128, 1024], replicated, may hold values from -0.5 to 0.5
- enc_query: bfloat16 [1024, 1024], P(None, 'head'), may hold values from -0.1875 to 0.1875
- enc_key: bfloat16 [1024, 1024], P(None, 'head'), may hold values from -0.1875 to 0.1875
- enc_value: bfloat16 [1024, 1024], P(None, 'head'), may hold values from -0.1875 to 0.1875
- enc_out: bfloat16 [1024, 1024], replicated, may hold values from -0.1875 to 0.1875
- proc_query: bfloat16 [1024, 1024], P(None, 'head'), may hold values from -0.1875 to 0.1875
- proc_key: bfloat16 [1024, 1024], P(None, 'head'), may hold values from -0.1875 to 0.1875
- proc_value: bfloat16 [1024, 1024], P(None, 'head'), may hold values from -0.1875 to 0.1875
- proc_out: bfloat16 [1024, 1024], P('head'), may hold values from -0.1875 to 0.1875
- mlp_gate: bfloat16 [1024, 4096], P(None, 'head'), may hold values from -0.1875 to 0.1875
- mlp_up: bfloat16 [1024, 4096], P(None, 'head'), may hold values from -0.1875 to 0.1875
- mlp_down: bfloat16 [4096, 1024], P('head'), may hold values from -0.09375 to 0.09375
Outputs:
- mesh_out: bfloat16 [16384, 1024], P('band')
Inputs may be any that keep to these rules, and one draw needn't show every extreme that they name: The live mesh nodes of band b are its first counts[b] slots; some band is full. `enc_edges`: A node of band b = n // 256 has its grid neighbours among grid points (b - 1) * 4096 to (b + 2) * 4096 - 1; in every band some edge reaches each end of that range that lies inside the grid.
All inputs are finite; a program needn't handle non-finite values.
Results may differ from a plain program's by a relative error of at most 0.02.
Values may be sent and summed in bfloat16 or wider, within the bound.
A program may use at most 192 MiB of HBM per device.

v0:
```python
import jax
import jax.numpy as jnp
from jax import lax
from jax.sharding import PartitionSpec as P

HDIM = 64


EPSILON = 1e-05
NEGATIVE = -1e30


def with_halo(array, sides, width):
    for axis, dim in sides:
        size, length = (lax.axis_size(axis), array.shape[dim])
        up = [(i, (i + 1) % size) for i in range(size - 1)]
        down = [(j, i) for i, j in up]
        last = lax.slice_in_dim(array, length - width, length, axis=dim)
        leading = lax.slice_in_dim(array, 0, width, axis=dim)
        before = lax.ppermute(last, axis, up)
        after = lax.ppermute(leading, axis, down)
        array = jnp.concatenate([before, array, after], axis=dim)
    return array


def normalize(source_rows):
    values_f = source_rows.astype(jnp.float32)
    centred = values_f - jnp.mean(values_f, -1, keepdims=True)
    variance = jnp.mean(centred * centred, -1, keepdims=True)
    return (centred * lax.rsqrt(variance + EPSILON)).astype(jnp.bfloat16)


def to_band(dense_scores, band_width):
    lead_dims = dense_scores.shape[:-2]
    row_count, col_count = dense_scores.shape[-2:]
    flattened = dense_scores.reshape(lead_dims + (row_count * col_count,))
    flattened = jnp.pad(flattened, [(0, 0)] * len(lead_dims) + [(0, row_count)])
    return flattened.reshape(lead_dims + (row_count, col_count + 1))[..., :band_width]


def from_band(banded, col_count):
    lead_dims = banded.shape[:-2]
    row_count, band_width = banded.shape[-2:]
    padded = jnp.pad(banded, [(0, 0)] * len(lead_dims) + [(0, 0), (0, col_count + 1 - band_width)])
    flattened = padded.reshape(lead_dims + (row_count * (col_count + 1),))[
        ..., : row_count * col_count
    ]
    return flattened.reshape(lead_dims + (row_count, col_count))


def local(
    grid_in,
    mesh_in,
    counts,
    enc_edges,
    enc_bias,
    proc_bias,
    w_embed,
    enc_query,
    enc_key,
    enc_value,
    enc_out,
    proc_query,
    proc_key,
    proc_value,
    proc_out,
    mlp_gate,
    mlp_up,
    mlp_down,
):
    band_index = lax.axis_index("band")
    band_count = lax.axis_size("band")
    grid_rows = grid_in.shape[0]
    node_rows, model_width = mesh_in.shape
    local_width = enc_query.shape[1]
    local_heads = local_width // HDIM
    edge_count = enc_edges.shape[0]
    score_scale = HDIM ** (-0.5)
    offsets = enc_edges - (band_index - 1) * grid_rows
    embedded = jnp.dot(grid_in, w_embed, preferred_element_type=jnp.float32).astype(jnp.bfloat16)
    key_rows = jnp.dot(embedded, enc_key, preferred_element_type=jnp.float32).astype(jnp.bfloat16)
    value_rows = jnp.dot(embedded, enc_value, preferred_element_type=jnp.float32).astype(
        jnp.bfloat16
    )
    key_rows, value_rows = (key_rows, value_rows)
    extended = with_halo(jnp.stack([key_rows, value_rows]), (("band", 1),), grid_rows)
    near_keys = extended[0][offsets].reshape(edge_count, node_rows, local_heads, HDIM)
    near_values = extended[1][offsets].reshape(edge_count, node_rows, local_heads, HDIM)
    mesh_query = jnp.dot(normalize(mesh_in), enc_query, preferred_element_type=jnp.float32).astype(
        jnp.bfloat16
    )
    mesh_query = mesh_query.reshape(node_rows, local_heads, HDIM)
    scores = jnp.einsum("knhc,nhc->khn", near_keys, mesh_query, preferred_element_type=jnp.float32)
    scores = scores * score_scale + enc_bias
    row_peak = jnp.max(scores, 0, keepdims=True)
    exponent = jnp.exp(scores - row_peak)
    weights = (exponent / jnp.sum(exponent, 0, keepdims=True)).astype(jnp.bfloat16)
    attended = jnp.einsum("khn,knhc->nhc", weights, near_values, preferred_element_type=jnp.float32)
    attended = attended.astype(jnp.bfloat16).reshape(node_rows, local_width)
    own_rows = lax.dynamic_slice_in_dim(
        enc_out, lax.axis_index("head") * local_width, local_width, 0
    )
    mixed = lax.psum(
        jnp.dot(attended, own_rows, preferred_element_type=jnp.float32).astype(jnp.bfloat16), "head"
    ).astype(jnp.float32)
    latent = (mesh_in.astype(jnp.float32) + mixed).astype(jnp.bfloat16)
    normed = normalize(latent)
    win_query = jnp.dot(normed, proc_query, preferred_element_type=jnp.float32).astype(jnp.bfloat16)
    win_key = jnp.dot(normed, proc_key, preferred_element_type=jnp.float32).astype(jnp.bfloat16)
    win_value = jnp.dot(normed, proc_value, preferred_element_type=jnp.float32).astype(jnp.bfloat16)
    window_width = proc_bias.shape[0]
    window_reach = (window_width - 1) // 2
    window_span = node_rows + 2 * window_reach
    neighbours = with_halo(jnp.stack([win_key, win_value]), (("band", 1),), window_reach)
    window_keys = neighbours[0].reshape(window_span, local_heads, HDIM)
    window_values = neighbours[1].reshape(window_span, local_heads, HDIM)
    dense_scores = jnp.einsum(
        "mhc,ehc->hme",
        win_query.reshape(node_rows, local_heads, HDIM),
        window_keys,
        preferred_element_type=jnp.float32,
    )
    banded = to_band(dense_scores * score_scale, window_width) + jnp.transpose(proc_bias, (1, 2, 0))
    key_offset = lax.iota(jnp.int32, window_width)[None, :] - window_reach
    key_position = band_index * node_rows + lax.iota(jnp.int32, node_rows)[:, None] + key_offset
    key_band = jnp.floor_divide(key_position, node_rows)
    own_count = counts[band_index]
    lower_count = counts[jnp.maximum(band_index - 1, 0)]
    upper_count = counts[jnp.minimum(band_index + 1, band_count - 1)]
    live_count = jnp.where(
        key_band < band_index, lower_count, jnp.where(key_band > band_index, upper_count, own_count)
    )
    key_live = key_position - key_band * node_rows < live_count
    inside = (key_position >= 0) & (key_position < band_count * node_rows)
    usable = (inside & (key_live | (key_offset == 0)))[None]
    masked = jnp.where(usable, banded, NEGATIVE)
    window_peak = jnp.max(masked, 2, keepdims=True)
    window_exp = jnp.where(usable, jnp.exp(masked - window_peak), 0.0)
    window_weights = (window_exp / jnp.sum(window_exp, 2, keepdims=True)).astype(jnp.bfloat16)
    dense_weights = from_band(window_weights, window_span)
    window_out = jnp.einsum(
        "hme,ehc->mhc", dense_weights, window_values, preferred_element_type=jnp.float32
    )
    window_out = window_out.astype(jnp.bfloat16).reshape(node_rows, local_width)
    gate_acts = jnp.dot(normed, mlp_gate, preferred_element_type=jnp.float32)
    up_acts = jnp.dot(normed, mlp_up, preferred_element_type=jnp.float32)
    hidden = (jax.nn.silu(gate_acts) * up_acts).astype(jnp.bfloat16)
    partial_value = jnp.dot(window_out, proc_out, preferred_element_type=jnp.float32)
    partial_value = partial_value + jnp.dot(hidden, mlp_down, preferred_element_type=jnp.float32)
    summed = lax.psum(partial_value.astype(jnp.bfloat16), "head").astype(jnp.float32)
    own_live = (lax.iota(jnp.int32, node_rows) < own_count).astype(jnp.float32)[:, None]
    return ((latent.astype(jnp.float32) + summed) * own_live).astype(jnp.bfloat16)


def solution(mesh):
    in_specs = (
        P("band", None),
        P("band", None),
        P(),
        P(None, "band"),
        P(None, "head", "band"),
        P(None, "head", "band"),
        P(),
        P(None, "head"),
        P(None, "head"),
        P(None, "head"),
        P(),
        P(None, "head"),
        P(None, "head"),
        P(None, "head"),
        P("head", None),
        P(None, "head"),
        P(None, "head"),
        P("head", None),
    )
    out_specs = P("band", None)
    return jax.shard_map(local, mesh=mesh, in_specs=in_specs, out_specs=out_specs, check_vma=False)
```

profile of v0, /device:TPU:97, one launch (start us, length us, event | category | flops | bytes accessed | tf_op | source)
XLA Modules:
  0.0 466.9 jit_solution(6340189628036916510)
XLA Ops:
  6.5 3.7 convolution_convert_fusion
  10.3 4.9 %fusion.1 = bf16[1,4096,512]{2,1,0:T(8,128)(2,1)S(1)} fusion(bf16[4096,1024]{1,0:T(8,128)(2,1)S(1)} %convolution_convert_fusion, bf16[1024,512]{1,0:T(8,128)(2,1)S(1)} %copy-done.8), kind=kOutput, calls=%fused_computation.12 | convolution fusion | flops 4297064448 | bytes 13631488 | tf_op jit(solution)/shard_map/dot_general | solution.py:81
  15.2 6.1 %fusion.2 = bf16[1,4096,512]{2,1,0:T(8,128)(2,1)} fusion(bf16[4096,1024]{1,0:T(8,128)(2,1)S(1)} %convolution_convert_fusion, bf16[1024,512]{1,0:T(8,128)(2,1)S(1)} %copy-done.9), kind=kOutput, calls=%fused_computation.13 | convolution fusion | flops 4297064448 | bytes 13631488 | tf_op jit(solution)/shard_map/dot_general | solution.py:82
  21.3 6.2 %pad_maximum_fusion.1 = bf16[2,4096,512]{2,1,0:T(8,128)(2,1)} fusion(bf16[1,4096,512]{2,1,0:T(8,128)(2,1)} %fusion.2, bf16[1,4096,512]{2,1,0:T(8,128)(2,1)S(1)} %fusion.1), kind=kLoop, calls=%fused_computation.6 | loop fusion | flops 4194304 | bytes 16777216 | tf_op jit(solution)/shard_map/stack | solution.py:86
  27.5 3.1 collective-permute-start
  30.7 6.9 %collective-permute-start.1 = (bf16[2,4096,512]{2,1,0:T(8,128)(2,1)}, bf16[2,4096,512]{2,1,0:T(8,128)(2,1)}, u32[]{:S(2)}, u32[]{:S(2)}) collective-permute-start(bf16[2,4096,512]{2,1,0:T(8,128)(2,1)} %pad_maximum_fusion.1), channel_id=1, source_target_pairs={{2,0},{4,2},{6,4},{8,6},{10,8},{12,10},{14,12},{16,14},{18,16},{20... | collective-permute-start | bytes 25165832 | tf_op jit(solution)/shard_map/ppermute | solution.py:21
  37.6 1.2 convert_reduce_fusion.1
  38.8 1.3 fusion.21
  40.2 1.9 convolution_convert_fusion.7
  42.2 3.4 copy.28
  46.2 169.1 %collective-permute-done = bf16[2,4096,512]{2,1,0:T(8,128)(2,1)} collective-permute-done((bf16[2,4096,512]{2,1,0:T(8,128)(2,1)}, bf16[2,4096,512]{2,1,0:T(8,128)(2,1)}, u32[]{:S(2)}, u32[]{:S(2)}) %collective-permute-start) | collective-permute-done | bytes 8388640 | tf_op jit(solution)/shard_map/ppermute | solution.py:20
  216.1 24.1 %pad_maximum_fusion = bf16[2,12288,512]{2,1,0:T(8,128)(2,1)} fusion(bf16[2,4096,512]{2,1,0:T(8,128)(2,1)} %collective-permute-done.1, bf16[1,4096,512]{2,1,0:T(8,128)(2,1)} %fusion.2, bf16[1,4096,512]{2,1,0:T(8,128)(2,1)} %copy-done.1, bf16[2,4096,512]{2,1,0:T(8,128)(2,1)} %collective-permute-done), kind=kLoop, calls=%fused_computation.3 | loop fusion | flops 100663296 | bytes 50331648 | tf_op jit(solution)/shard_map/concatenate | solution.py:22
  240.3 16.9 %slice_bitcast_fusion = (bf16[12288,512]{1,0:T(8,128)(2,1)}, bf16[12288,512]{1,0:T(8,128)(2,1)}) fusion(bf16[2,12288,512]{2,1,0:T(8,128)(2,1)} %pad_maximum_fusion), kind=kLoop, calls=%fused_computation.4 | loop fusion | bytes 50331648 | tf_op jit(solution)/shard_map/squeeze | solution.py:88
  257.2 19.5 %gather_fusion = bf16[3072,512]{1,0:T(8,128)(2,1)} fusion(bf16[12288,512]{1,0:T(8,128)(2,1)} %get-tuple-element.10, s32[3072]{0:T(1024)S(1)} %broadcast_clamp_fusion), kind=kCustom, calls=%fused_computation | custom fusion | bytes 6303744 | tf_op jit(solution)/shard_map/gather | solution.py:87
  276.7 4.7 %copy.23 = bf16[3072,512]{0,1:T(8,128)(2,1)} copy(bf16[3072,512]{1,0:T(8,128)(2,1)} %gather_fusion) | data formatting | bytes 6291456 | tf_op jit(solution)/shard_map/gather | solution.py:87
  281.4 6.8 %reshape.145 = bf16[12,256,8,64]{1,0,3,2:T(8,128)(2,1)} reshape(bf16[3072,512]{0,1:T(8,128)(2,1)} %copy.23) | data formatting | bytes 6291456 | tf_op jit(solution)/shard_map/reshape | solution.py:87
  288.1 3.2 multiply_reduce_fusion.1
  291.5 19.5 %gather_fusion.1 = bf16[3072,512]{1,0:T(8,128)(2,1)} fusion(bf16[12288,512]{1,0:T(8,128)(2,1)} %get-tuple-element.9, s32[3072]{0:T(1024)S(1)} %broadcast_clamp_fusion), kind=kCustom, calls=%fused_computation.1 | custom fusion | bytes 6303744 | tf_op jit(solution)/shard_map/gather | solution.py:88
  311.1 4.7 %copy.24 = bf16[3072,512]{0,1:T(8,128)(2,1)} copy(bf16[3072,512]{1,0:T(8,128)(2,1)} %gather_fusion.1) | data formatting | bytes 6291456 | tf_op jit(solution)/shard_map/gather | solution.py:88
  315.8 6.9 %reshape.146 = bf16[12,256,8,64]{1,0,3,2:T(8,128)(2,1)} reshape(bf16[3072,512]{0,1:T(8,128)(2,1)} %copy.24) | data formatting | bytes 6291456 | tf_op jit(solution)/shard_map/reshape | solution.py:88
  322.7 4.2 multiply_reduce_fusion
  326.9 1.3 convolution_convert_fusion.3
  328.3 2.3 fusion.40
  330.6 26.1 %all-reduce.5.cloned.1.call-done = bf16[256,1024]{1,0:T(8,128)(2,1)} async-done(((bf16[256,1024]{1,0:T(8,128)(2,1)}), bf16[256,1024]{1,0:T(8,128)(2,1)}) %all-reduce.5.cloned.1.call-update) | async-done | bytes 524304 | tf_op jit(solution)/shard_map/psum | solution.py:103
  356.7 1.4 convert_reduce_fusion
  358.4 1.7 fusion.17
  360.2 1.7 fusion.16
  362.7 3.1 collective-permute-start.2
  365.8 6.4 %collective-permute-start.3 = (bf16[2,128,512]{2,1,0:T(8,128)(2,1)}, bf16[2,128,512]{2,1,0:T(8,128)(2,1)}, u32[]{:S(2)}, u32[]{:S(2)}) collective-permute-start(bf16[2,128,512]{2,1,0:T(8,128)(2,1)} %get-tuple-element.14), channel_id=1, source_target_pairs={{2,0},{4,2},{6,4},{8,6},{10,8},{12,10},{14,12},{16,14},{18,16},{20... | collective-permute-start | bytes 786440 | tf_op jit(solution)/shard_map/ppermute | solution.py:21
  372.3 2.7 fusion.48
  375.0 7.6 %fusion.18 = f32[256,1024]{1,0:T(8,128)} fusion(bf16[2048,1024]{1,0:T(8,128)(2,1)} %param.35, bf16[1024,2048]{1,0:T(8,128)(2,1)} %param.34, f32[256,2048]{1,0:T(8,128)} %fusion.48, bf16[256,1024]{1,0:T(8,128)(2,1)S(1)} %get-tuple-element.6, f32[256]{0:T(256)S(1)} %add_rsqrt_fusion, f32[256]{0:T(256)S(1)} %broadcast_multiply_fusion), kind=kOutput, calls=%fused_computation.51 | convolution fusion | flops 2151677952 | bytes 12060672 | tf_op jit(solution)/shard_map/dot_general | solution.py:149
  382.6 2.4 convolution_convert_fusion.4
  385.0 1.1 copy.26
  386.1 1.1 pad_maximum_fusion.2
  387.2 1.1 fusion.55
  388.3 1.3 copy.27
  390.3 2.4 copy.46
  392.8 2.4 pad.8
  395.1 9.2 %reshape.150 = f32[8,256,513]{2,1,0:T(8,128)} reshape(f32[8,131328]{1,0:T(8,128)} %pad.8) | data formatting | bytes 8404992 | tf_op jit(solution)/shard_map/reshape | solution.py:38
  404.3 8.4 %fusion.57 = (f32[8,256]{1,0:T(8,128)S(1)}, f32[8,256,257]{2,1,0:T(8,128)S(1)}) fusion(f32[8,256,513]{2,1,0:T(8,128)} %reshape.150, f32[257,8,256]{0,2,1:T(8,128)} %copy.28, pred[256,257]{1,0:T(8,128)(4,1)S(1)} %fusion.40), kind=kOutput, calls=%fused_computation.104 | output fusion | flops 2631936 | bytes 8601600 | tf_op jit(solution)/shard_map/sub | solution.py:138
  413.0 1.8 pad.9
  414.9 6.2 %reshape.180 = bf16[1050624]{0:T(1024)(128)(2,1)} reshape(bf16[8,256,513]{2,1,0:T(8,128)(2,1)} %pad.9) | data formatting | bytes 4202496
  421.1 5.2 %reshape.151 = bf16[8,131328]{1,0:T(8,128)(2,1)} reshape(bf16[1050624]{0:T(1024)(128)(2,1)} %reshape.180) | data formatting | bytes 4202496 | tf_op jit(solution)/shard_map/reshape | solution.py:45
  426.3 3.0 slice.43
  430.3 2.6 fusion.13
  432.9 2.8 fusion.8
  436.3 21.6 %all-reduce.7.cloned.1.call-done = bf16[256,1024]{1,0:T(8,128)(2,1)} async-done(((bf16[256,1024]{1,0:T(8,128)(2,1)}), bf16[256,1024]{1,0:T(8,128)(2,1)}) %all-reduce.7.cloned.1.call-update) | async-done | bytes 524304 | tf_op jit(solution)/shard_map/psum | solution.py:150
  457.8 2.0 fusion.25
  (50 shorter events, 5.8 us)
Async XLA Ops:
  6.5 320.4 %copy-start = (bf16[1024,1024]{1,0:T(8,128)(2,1)S(1)}, bf16[1024,1024]{1,0:T(8,128)(2,1)}, u32[]{:S(2)}) copy-start(bf16[1024,1024]{1,0:T(8,128)(2,1)} %param.28) | copy-start | bytes 6291460
  6.5 350.2 %all-reduce.5.cloned.1.call-start = ((), (), s32[]{:S(2)}) async-start(), calls=%async_computation | async-start | bytes 1048576 | tf_op jit(solution)/shard_map/psum | solution.py:103
  6.5 3.8 copy-start.8
  10.3 4.9 %copy-start.9 = (bf16[1024,512]{1,0:T(8,128)(2,1)S(1)}, bf16[1024,512]{1,0:T(8,128)(2,1)}, u32[]{:S(2)}) copy-start(bf16[1024,512]{1,0:T(8,128)(2,1)} %param.27) | copy-start | bytes 3145732
  15.2 6.1 %copy-start.1 = (bf16[1,4096,512]{2,1,0:T(8,128)(2,1)}, bf16[1,4096,512]{2,1,0:T(8,128)(2,1)S(1)}, u32[]{:S(2)}) copy-start(bf16[1,4096,512]{2,1,0:T(8,128)(2,1)S(1)} %fusion.1) | copy-start | bytes 12582916
  21.3 16.2 %copy-start.5 = (s32[12,256]{1,0:T(8,128)S(1)}, s32[12,256]{1,0:T(8,128)}, u32[]{:S(2)}) copy-start(s32[12,256]{1,0:T(8,128)} %param.21) | copy-start | bytes 36868
  27.5 187.7 %collective-permute-start = (bf16[2,4096,512]{2,1,0:T(8,128)(2,1)}, bf16[2,4096,512]{2,1,0:T(8,128)(2,1)}, u32[]{:S(2)}, u32[]{:S(2)}) collective-permute-start(bf16[2,4096,512]{2,1,0:T(8,128)(2,1)} %pad_maximum_fusion.1), channel_id=1, source_target_pairs={{0,2},{2,4},{4,6},{6,8},{8,10},{10,12},{12,14},{14,16},{16,18},{18... | collective-permute-start | bytes 25165832 | tf_op jit(solution)/shard_map/ppermute | solution.py:20
  30.7 185.5 %collective-permute-start.1 = (bf16[2,4096,512]{2,1,0:T(8,128)(2,1)}, bf16[2,4096,512]{2,1,0:T(8,128)(2,1)}, u32[]{:S(2)}, u32[]{:S(2)}) collective-permute-start(bf16[2,4096,512]{2,1,0:T(8,128)(2,1)} %pad_maximum_fusion.1), channel_id=1, source_target_pairs={{2,0},{4,2},{6,4},{8,6},{10,8},{12,10},{14,12},{16,14},{18,16},{20... | collective-permute-start | bytes 25165832 | tf_op jit(solution)/shard_map/ppermute | solution.py:21
  38.8 6.7 %copy-start.6 = (s32[64]{0:T(128)S(1)}, s32[64]{0:T(128)}, u32[]{:S(2)}) copy-start(s32[64]{0:T(128)} %param.20) | copy-start | bytes 772
  288.1 3.2 copy-start.4
  322.7 34.0 %copy-start.2 = (bf16[256,1024]{1,0:T(8,128)(2,1)S(1)}, bf16[256,1024]{1,0:T(8,128)(2,1)}, u32[]{:S(2)}) copy-start(bf16[256,1024]{1,0:T(8,128)(2,1)} %param.19) | copy-start | bytes 1572868
  328.2 129.6 %all-reduce.7.cloned.1.call-start = ((), (), s32[]{:S(2)}) async-start(), calls=%async_computation.1 | async-start | bytes 1048576 | tf_op jit(solution)/shard_map/psum | solution.py:150
  356.7 15.5 %copy-start.7 = (bf16[1024,2048]{1,0:T(8,128)(2,1)S(1)}, bf16[1024,2048]{1,0:T(8,128)(2,1)}, u32[]{:S(2)}) copy-start(bf16[1024,2048]{1,0:T(8,128)(2,1)} %param.33) | copy-start | bytes 12582916
  362.7 23.4 %collective-permute-start.2 = (bf16[2,128,512]{2,1,0:T(8,128)(2,1)}, bf16[2,128,512]{2,1,0:T(8,128)(2,1)}, u32[]{:S(2)}, u32[]{:S(2)}) collective-permute-start(bf16[2,128,512]{2,1,0:T(8,128)(2,1)} %get-tuple-element.13), channel_id=1, source_target_pairs={{0,2},{2,4},{4,6},{6,8},{8,10},{10,12},{12,14},{14,16},{16,18},{18... | collective-permute-start | bytes 786440 | tf_op jit(solution)/shard_map/ppermute | solution.py:20
  365.8 20.3 %collective-permute-start.3 = (bf16[2,128,512]{2,1,0:T(8,128)(2,1)}, bf16[2,128,512]{2,1,0:T(8,128)(2,1)}, u32[]{:S(2)}, u32[]{:S(2)}) collective-permute-start(bf16[2,128,512]{2,1,0:T(8,128)(2,1)} %get-tuple-element.14), channel_id=1, source_target_pairs={{2,0},{4,2},{6,4},{8,6},{10,8},{12,10},{14,12},{16,14},{18,16},{20... | collective-permute-start | bytes 786440 | tf_op jit(solution)/shard_map/ppermute | solution.py:21
  421.0 8.3 %copy-start.3 = (bf16[1,512,512]{2,1,0:T(8,128)(2,1)S(1)}, bf16[1,512,512]{2,1,0:T(8,128)(2,1)}, u32[]{:S(2)}) copy-start(bf16[1,512,512]{2,1,0:T(8,128)(2,1)} %get-tuple-element.12) | copy-start | bytes 1572868
Sparse Core Ops, SparseCore 0:
  328.3 28.3 all-reduce.4
  435.8 21.9 all-reduce.6
where the time goes:
time: 476 us; the launch traced here: 467 us
  waiting for transfers between devices  218 us (46%)
  local copies, waits for them, and re-layouts  118 us (25%)
  other arithmetic  57.7 us (12%)
  matrix products  40.2 us (8%)
  starting transfers between devices  19.6 us (4%)
  between operations  14 us (3%)
    ppermute x2, waiting for transfers between devices, with_halo(): before = lax.ppermute(last, axis, up)  169 us
    psum x1, waiting for transfers between devices, local(): lax.psum(jnp.dot(attended, own_rows, preferred_element_type=jnp.float32)....  26.1 us
    concatenate x2, other arithmetic, with_halo(): array = jnp.concatenate([before, array, after], axis=dim)  25.2 us
    gather x2, local copies, waits for them, and re-layouts, local(): extended[1][offsets].reshape(edge_count, node_rows, local_heads, HDIM)  24.2 us
    gather x2, local copies, waits for them, and re-layouts, local(): extended[0][offsets].reshape(edge_count, node_rows, local_heads, HDIM)  24.2 us
    psum x1, waiting for transfers between devices, local(): lax.psum(partial_value.astype(jnp.bfloat16), 'head').astype(jnp.float32)  21.6 us
    squeeze x1, local copies, waits for them, and re-layouts, local(): extended[1][offsets].reshape(edge_count, node_rows, local_heads, HDIM)  16.9 us
    ppermute x2, starting transfers between devices, with_halo(): after = lax.ppermute(leading, axis, down)  13.3 us
  transfers between devices with their start and end apart: 6, of which 4 were waited for; matrix products, arithmetic and copies ran while one was open for 5% of the time, Pallas kernels for 0%

commit v1 on v0

v1 whole, which is shorter than its diff:
```python
import jax
import jax.numpy as jnp
from jax import lax
from jax.experimental import pallas as pl
from jax.experimental.pallas import tpu as pltpu
from jax.sharding import PartitionSpec as P

HDIM = 64
EPSILON = 1e-05
NEGATIVE = -1e30
F32 = jnp.float32
BF16 = jnp.bfloat16
LANES = 128
BLOCK = 16
CHUNKS = 4
VMEM_BYTES = 60 * 1024 * 1024


def nn(left, right):
    return lax.dot_general(left, right, (((1,), (0,)), ((), ())), preferred_element_type=F32)


def nt(left, right):
    return lax.dot_general(left, right, (((1,), (1,)), ((), ())), preferred_element_type=F32)


def iota(shape, dim):
    return lax.broadcasted_iota(jnp.int32, shape, dim)


def normalize(rows):
    centred = rows - jnp.mean(rows, -1, keepdims=True)
    variance = jnp.mean(centred * centred, -1, keepdims=True)
    return (centred * lax.rsqrt(variance + EPSILON)).astype(BF16)


def kernel(
    edge_s, count_s, grid, mesh_in, enc_bias, proc_bias, w_embed,
    enc_query, enc_key, enc_value, enc_out,
    proc_query, proc_key, proc_value, proc_out, mlp_gate, mlp_up, mlp_down,
    out,
    ext, extf, mesh_v, we_v, eq_v, ek_v, ev_v, eo_v, pq_v, pk_v, pv_v, po_v,
    gate_v, up_v, down_v, eb_v, pb_v, bd, qk, wv, g, u_s, lat, nx, q_s, k_s, v_s,
    hid, part, wo, psend, precv, ob,
    load_sem, gs_sem, gr_sem, fs_sem, fr_sem, xs_sem, xr_sem, ls_sem, lr_sem,
    hs_sem, hr_sem, ps_sem, pr_sem, os_sem,
):
    band, core = lax.axis_index("band"), lax.axis_index("head")
    bands = lax.axis_size("band")
    other = 1 - core
    left = lax.rem(band + bands - 1, bands)
    right = lax.rem(band + 1, bands)
    toward = jnp.where(core == 1, right, left)
    grid_rows = grid.shape[0]
    nodes = mesh_in.shape[0]
    half = nodes // 2
    width = mesh_in.shape[1]
    local_width = enc_query.shape[1]
    local_heads = local_width // HDIM
    pairs = local_heads // 2
    edges = edge_s.shape[0]

    def mesh_id(b, h):
        return {"band": b, "head": h}

    own = pl.ds(pl.multiple_of(core * local_width, LANES), local_width)
    theirs = pl.ds(pl.multiple_of(other * local_width, LANES), local_width)
    bias_rows = enc_bias.shape[0]
    sources = [
        (mesh_in, mesh_v),
        (enc_query, eq_v),
        (w_embed, we_v),
        (enc_key, ek_v),
        (enc_value, ev_v),
        (enc_bias.at[:, pl.ds(0, half)], eb_v.at[0, pl.ds(0, bias_rows)]),
        (enc_bias.at[:, pl.ds(half, half)], eb_v.at[1, pl.ds(0, bias_rows)]),
        (proc_bias.at[:, pl.ds(0, half)], pb_v.at[0]),
        (proc_bias.at[:, pl.ds(half, half)], pb_v.at[1]),
        (grid, ext.at[pl.ds(grid_rows, grid_rows)]),
        (enc_out.at[own], eo_v.at[pl.ds(0, local_width)]),
        (enc_out.at[theirs], eo_v.at[pl.ds(local_width, local_width)]),
        (mlp_gate, gate_v),
        (mlp_up, up_v),
        (proc_query, pq_v),
        (proc_key, pk_v),
        (proc_value, pv_v),
        (mlp_down, down_v),
        (proc_out, po_v),
    ]
    loads = [
        pltpu.make_async_copy(src, dst, load_sem.at[i]) for i, (src, dst) in enumerate(sources)
    ]
    (
        l_mesh, l_eq, l_we, l_ek, l_ev, l_eb0, l_eb1, l_pb0, l_pb1, l_grid, l_eo0, l_eo1,
        l_gate, l_up, l_pq, l_pk, l_pv, l_down, l_po,
    ) = loads
    for load in loads[:9]:
        load.start()

    barrier = pltpu.get_barrier_semaphore()
    for partner in (
        mesh_id(band, other), mesh_id(left, core), mesh_id(right, core), mesh_id(toward, other)
    ):
        pl.semaphore_signal(
            barrier, inc=1, device_id=partner, device_id_type=pl.DeviceIdType.MESH
        )
    pl.semaphore_wait(barrier, 4)

    def remote(src, dst, send, recv, device):
        return pltpu.make_async_remote_copy(
            src_ref=src, dst_ref=dst, send_sem=send, recv_sem=recv,
            device_id=device, device_id_type=pl.DeviceIdType.MESH,
        )

    piece = grid_rows // 2 // CHUNKS
    halo = []
    passed = []
    for k in range(CHUNKS):
        src_row = pl.multiple_of(core * (grid_rows // 2) + k * piece, piece)
        far_row = pl.multiple_of(other * (grid_rows // 2) + k * piece, piece)
        for d, device in ((0, right), (1, left)):
            start = 2 * grid_rows * d
            slot = d * CHUNKS + k
            halo.append(
                remote(
                    grid.at[pl.ds(src_row, piece)],
                    ext.at[pl.ds(pl.multiple_of(start + src_row, piece), piece)],
                    gs_sem.at[slot], gr_sem.at[slot], mesh_id(device, core),
                )
            )
            here = ext.at[pl.ds(pl.multiple_of(start + src_row, piece), piece)]
            passed.append(
                remote(here, here, fs_sem.at[slot], fr_sem.at[slot], mesh_id(band, other))
            )
    for copy in halo:
        copy.start()
    for load in loads[9:]:
        load.start()

    padding = eb_v.shape[1] - bias_rows
    eb_v[:, pl.ds(bias_rows, padding), :] = jnp.zeros((2, padding, half), F32)
    l_mesh.wait()
    normed_mesh = normalize(mesh_v[...].astype(F32))
    l_eq.wait()
    queries = nn(normed_mesh, eq_v[...]).astype(BF16)
    queries = (queries.astype(F32) * HDIM**-0.5).astype(BF16)
    l_we.wait()
    l_ek.wait()
    key_map = nn(we_v[...], ek_v[...]).astype(BF16)
    l_ev.wait()
    wv[0] = nn(we_v[...], ev_v[...]).astype(BF16)
    l_eb0.wait()
    l_eb1.wait()
    low_half = iota((nodes, LANES), 1) < HDIM
    for h in range(local_heads):
        columns = slice(h // 2 * LANES, (h // 2 + 1) * LANES)
        keep = low_half if h % 2 == 0 else jnp.logical_not(low_half)
        masked = jnp.where(keep, queries[:, columns].astype(F32), 0.0).astype(BF16)
        mapped = nt(masked, key_map[:, columns]).astype(BF16)
        for n in range(2):
            bias = eb_v[n, pl.ds(h, 16, stride=local_heads), :]
            high = bias.astype(BF16).astype(F32)
            middle = (bias - high).astype(BF16).astype(F32)
            low = (bias - high) - middle
            lanes = jnp.concatenate([high, middle, low, jnp.zeros((LANES - 48, half), F32)], 0)
            slot = lax.rem(core + n, 2)
            qk[slot, h, :, 0:LANES] = mapped[n * half : (n + 1) * half]
            qk[slot, h, :, LANES : 2 * LANES] = lanes.T.astype(BF16)
    exchange = [
        remote(qk.at[1], qk.at[2], xs_sem.at[0], xr_sem.at[0], mesh_id(band, other)),
        remote(wv.at[0], wv.at[1], xs_sem.at[1], xr_sem.at[1], mesh_id(band, other)),
    ]
    for copy in exchange:
        copy.start()

    reach = half
    span = nodes + 2 * reach
    window = 3 * half
    own_count = count_s[band]
    lower_count = jnp.where(band > 0, count_s[left], 0)
    upper_count = jnp.where(band < bands - 1, count_s[right], 0)
    key_slot = iota((1, span), 1)
    before, after = key_slot < reach, key_slot >= reach + nodes
    limit = jnp.where(before, lower_count, jnp.where(after, upper_count, own_count))
    place = key_slot - jnp.where(before, reach - nodes, jnp.where(after, reach + nodes, reach))
    live = jnp.where(place < limit, 1, 0)
    offset = iota((half, window), 1) - iota((half, window), 0)
    in_window = (offset >= 0) & (offset <= 2 * reach)
    l_pb0.wait()
    l_pb1.wait()
    last = [pb_v[i, pl.ds(2 * reach * local_heads, local_heads), :].T for i in range(2)]

    def window_bias(h):
        for i in range(2):
            turned = pb_v[i, pl.ds(h, 2 * reach, stride=local_heads), :].T
            wide = jnp.concatenate([turned, jnp.zeros((half, window - 2 * reach), F32)], 1)
            skewed = pltpu.roll(wide, 0, 1, stride=1, stride_axis=0)
            final = last[i][:, h : h + 1]
            skewed = jnp.where(offset == 2 * reach, final, skewed)
            usable = in_window & (
                (live[:, i * half : i * half + window] > 0) | (offset == reach)
            )
            bd[h, i] = jnp.where(usable, skewed, NEGATIVE)

    def widen(k, d, which):
        start = pl.multiple_of(
            2 * grid_rows * d + which * (grid_rows // 2) + k * piece, piece
        )
        rows = pl.ds(start, piece)
        extf[rows, :] = ext[rows, :].astype(F32)

    v_s[...] = jnp.ones(v_s.shape, BF16)
    g[...] = jnp.zeros(g.shape, F32)
    l_grid.wait()
    for k in range(CHUNKS):
        for h in range(k * local_heads // CHUNKS, (k + 1) * local_heads // CHUNKS):
            window_bias(h)
        own_rows = pl.ds(grid_rows + k * 2 * piece, 2 * piece)
        extf[own_rows, :] = ext[own_rows, :].astype(F32)
        for d in range(2):
            halo[2 * k + d].wait_recv()
            passed[2 * k + d].start()
        for d in range(2):
            widen(k, d, core)
        if k > 0:
            for d in range(2):
                passed[2 * (k - 1) + d].wait_recv()
                widen(k - 1, d, other)
    for d in range(2):
        passed[2 * (CHUNKS - 1) + d].wait_recv()
        widen(CHUNKS - 1, d, other)

    base = (band - 1) * grid_rows
    blocks = half // BLOCK
    block_rows = 16 * BLOCK

    def gather(i, carry):
        block, edge = i // edges, lax.rem(i, edges)
        for n in range(BLOCK):
            row = jnp.maximum(edge_s[edge, core * half + block * BLOCK + n] - base, 0)
            g[pl.ds(block * block_rows + edge * BLOCK + n, 1), :] = extf[pl.ds(row, 1), :]
        return carry

    lax.fori_loop(0, blocks * edges, gather, 0)

    for copy in exchange:
        copy.wait()
    lane = iota((block_rows, LANES), 1)
    edge_of_row = iota((block_rows, LANES), 0) // BLOCK
    marks = (lane < 48) & (lax.rem(lane, 16) == edge_of_row)
    marks = marks.astype(F32).astype(BF16)
    ones = jnp.ones((block_rows, LANES), BF16)
    row = iota((block_rows, block_rows), 0)
    column = iota((block_rows, block_rows), 1)
    same = (lax.rem(row, BLOCK) == lax.rem(column, BLOCK)) & (column < edges * BLOCK)
    for block in range(blocks):
        rows = slice(block * BLOCK, (block + 1) * BLOCK)
        near = g[block * block_rows : (block + 1) * block_rows, :].astype(BF16)
        asked = jnp.concatenate(
            [qk[s, :, rows, :].reshape(local_heads * BLOCK, 2 * LANES) for s in (0, 2)], 0
        )
        scores = jnp.where(same, nt(asked, jnp.concatenate([near, marks], 1)), NEGATIVE)
        peak = jnp.max(scores, 1, keepdims=True)
        weights = jnp.exp(scores - peak).astype(BF16)
        mixed = nn(weights, jnp.concatenate([near, ones], 1))
        mixed = (mixed[:, :LANES] / mixed[:, LANES:]).astype(BF16)
        for h in range(2 * local_heads):
            u_s[rows, h * LANES : (h + 1) * LANES] = mixed[h * BLOCK : (h + 1) * BLOCK]
    low_lanes = iota((LANES, LANES), 1) < HDIM
    attended = []
    for pair in range(2 * pairs):
        value_map = wv[pair // pairs, :, pair % pairs * LANES : (pair % pairs + 1) * LANES]
        value_map = value_map.astype(F32)
        value_map = jnp.concatenate(
            [jnp.where(low_lanes, value_map, 0.0), jnp.where(low_lanes, 0.0, value_map)], 0
        ).astype(BF16)
        attended.append(nn(u_s[:, pair * 2 * LANES : (pair + 1) * 2 * LANES], value_map))
    attended = jnp.concatenate(attended, 1).astype(BF16)
    l_eo0.wait()
    l_eo1.wait()
    own_mesh = mesh_v[pl.ds(pl.multiple_of(core * half, half), half), :].astype(F32)
    latent = (own_mesh + nn(attended, eo_v[...])).astype(BF16)
    lat[core] = latent
    to_sibling = remote(lat.at[core], lat.at[core], ls_sem.at[0], lr_sem.at[0], mesh_id(band, other))
    to_sibling.start()
    nx[1 + core] = normalize(latent.astype(F32))
    slot = 3 * other
    sends = [
        remote(nx.at[1 + core], nx.at[slot], hs_sem.at[0], hr_sem.at[slot], mesh_id(toward, core)),
        remote(nx.at[1 + core], nx.at[slot], hs_sem.at[1], hr_sem.at[slot], mesh_id(toward, other)),
    ]
    for copy in sends:
        copy.start()
    to_sibling.wait_recv()
    nx[2 - core] = normalize(lat[other].astype(F32))
    normed = nx[1:3].reshape(nodes, width)

    l_gate.wait()
    l_up.wait()
    step = 512
    for ch in range(gate_v.shape[1] // step):
        columns = slice(ch * step, (ch + 1) * step)
        gated = nn(normed, gate_v[:, columns])
        raised = nn(normed, up_v[:, columns])
        hid[:, columns] = (0.5 * gated * (1.0 + jnp.tanh(0.5 * gated)) * raised).astype(BF16)
    l_pq.wait()
    win_query = nn(normed, pq_v[...]).astype(BF16)
    q_s[...] = (win_query.astype(F32) * HDIM**-0.5).astype(BF16)
    l_pk.wait()
    l_pv.wait()

    def keys_values(rows, source):
        k_s[rows, :] = nn(source, pk_v[...]).astype(BF16)
        values = nn(source, pv_v[...]).astype(BF16)
        for pair in range(pairs):
            v_s[rows, pair * 2 * LANES : pair * 2 * LANES + LANES] = values[
                :, pair * LANES : (pair + 1) * LANES
            ]

    keys_values(slice(reach, reach + nodes), normed)
    l_down.wait()
    for ch in range(width // step):
        columns = slice(ch * step, (ch + 1) * step)
        part[:, columns] = nn(hid[...], down_v[:, columns])

    for s, at in ((0, 0), (3, reach + nodes)):
        remote(
            nx.at[s], nx.at[s], hs_sem.at[0], hr_sem.at[s], mesh_id(toward, core)
        ).wait_recv()
        keys_values(slice(at, at + reach), nx[s])

    l_po.wait()
    results = []
    first_head = iota((half, LANES), 1) < HDIM
    for i in range(2):
        rows = slice(i * half, (i + 1) * half)
        seen = slice(i * half, i * half + window)
        for pair in range(pairs):
            columns = slice(pair * LANES, (pair + 1) * LANES)
            asked = q_s[rows, columns].astype(F32)
            keys = k_s[seen, columns]
            values = v_s[seen, pair * 2 * LANES : (pair + 1) * 2 * LANES]
            outs = []
            for h in range(2):
                keep = first_head if h == 0 else jnp.logical_not(first_head)
                masked = jnp.where(keep, asked, 0.0).astype(BF16)
                scores = nt(masked, keys) + bd[pair * 2 + h, i]
                peak = jnp.max(scores, 1, keepdims=True)
                weights = jnp.exp(scores - peak).astype(BF16)
                mixed = nn(weights, values)
                outs.append(mixed[:, :LANES] / mixed[:, LANES:])
            wo[rows, columns] = jnp.where(first_head, outs[0], outs[1]).astype(BF16)
        psend[i] = (part[rows, :] + nn(wo[rows, :], po_v[...])).astype(BF16)
        result = remote(
            psend.at[i], precv.at[i], ps_sem.at[i], pr_sem.at[i], mesh_id(band, other)
        )
        result.start()
        results.append(result)
    stores = []
    for i in range(2):
        results[i].wait_recv()
        summed = psend[i].astype(F32) + precv[i].astype(F32)
        node = iota((half, width), 0) + i * half
        scale = (node < own_count).astype(F32)
        ob[i] = ((lat[i].astype(F32) + summed) * scale).astype(BF16)
        store = pltpu.make_async_copy(ob.at[i], out.at[pl.ds(i * half, half)], os_sem.at[i])
        store.start()
        stores.append(store)
    for copy in halo + passed + [to_sibling] + sends + results:
        copy.wait_send()
    for store in stores:
        store.wait()


def local(
    grid_in, mesh_in, counts, enc_edges, enc_bias, proc_bias, w_embed, enc_query, enc_key,
    enc_value, enc_out, proc_query, proc_key, proc_value, proc_out, mlp_gate, mlp_up, mlp_down,
):
    grid_rows, channels = grid_in.shape
    nodes, width = mesh_in.shape
    local_width = enc_query.shape[1]
    heads = local_width // HDIM
    hidden = mlp_gate.shape[1]
    half = nodes // 2
    edges = enc_edges.shape[0]
    enc_bias = enc_bias.reshape(edges * heads, nodes)
    proc_bias = proc_bias.reshape(-1, nodes)
    anywhere = pl.BlockSpec(memory_space=pl.ANY)
    in_scalar = pl.BlockSpec(memory_space=pltpu.SMEM)
    dma = pltpu.SemaphoreType.DMA
    vmem = pltpu.VMEM
    scratch = [
        vmem((3 * grid_rows, channels), BF16),
        vmem((3 * grid_rows, channels), F32),
        vmem((nodes, width), BF16),
        vmem((channels, width), BF16),
        vmem((width, local_width), BF16),
        vmem((width, local_width), BF16),
        vmem((width, local_width), BF16),
        vmem((width, width), BF16),
        vmem((width, local_width), BF16),
        vmem((width, local_width), BF16),
        vmem((width, local_width), BF16),
        vmem((local_width, width), BF16),
        vmem((width, hidden), BF16),
        vmem((width, hidden), BF16),
        vmem((hidden, width), BF16),
        vmem((2, 16 * heads, half), F32),
        vmem((2, proc_bias.shape[0], half), F32),
        vmem((heads, 2, half, 3 * half), F32),
        vmem((3, heads, half, 2 * LANES), BF16),
        vmem((2, channels, local_width), BF16),
        vmem((half * 16, channels), F32),
        vmem((half, 2 * heads * channels), BF16),
        vmem((2, half, width), BF16),
        vmem((4, half, width), BF16),
        vmem((nodes, local_width), BF16),
        vmem((2 * nodes, local_width), BF16),
        vmem((2 * nodes, 2 * local_width), BF16),
        vmem((nodes, hidden), BF16),
        vmem((nodes, width), F32),
        vmem((nodes, local_width), BF16),
        vmem((2, half, width), BF16),
        vmem((2, half, width), BF16),
        vmem((2, half, width), BF16),
        dma((19,)),
        dma((2 * CHUNKS,)),
        dma((2 * CHUNKS,)),
        dma((2 * CHUNKS,)),
        dma((2 * CHUNKS,)),
        dma((2,)),
        dma((2,)),
        dma((1,)),
        dma((1,)),
        dma((2,)),
        dma((4,)),
        dma((2,)),
        dma((2,)),
        dma((2,)),
    ]
    return pl.pallas_call(
        kernel,
        out_shape=jax.ShapeDtypeStruct((nodes, width), BF16),
        in_specs=[in_scalar, in_scalar] + [anywhere] * 16,
        out_specs=anywhere,
        scratch_shapes=scratch,
        compiler_params=pltpu.CompilerParams(
            collective_id=0, has_side_effects=True, vmem_limit_bytes=VMEM_BYTES
        ),
        name="encoder_processor",
    )(
        enc_edges, counts, grid_in, mesh_in, enc_bias, proc_bias, w_embed, enc_query, enc_key,
        enc_value, enc_out, proc_query, proc_key, proc_value, proc_out, mlp_gate, mlp_up, mlp_down,
    )


def solution(mesh):
    heads = P(None, "head")
    in_specs = (
        P("band", None), P("band", None), P(), P(None, "band"), P(None, "head", "band"),
        P(None, "head", "band"), P(), heads, heads, heads, P(), heads, heads, heads,
        P("head", None), heads, heads, P("head", None),
    )
    return jax.shard_map(
        local, mesh=mesh, in_specs=in_specs, out_specs=P("band", None), check_vma=False
    )
```

time: 476 us -> 54.6 us (0.11)
  the two profiles are of different devices: /device:TPU:97 before, /device:TPU:1 now
where the time goes in v1:
time: 54.6 us; the launch traced here: 54.4 us
  Pallas kernels  52.5 us (96%)
  local copies, waits for them, and re-layouts  1.87 us (3%)
    pallas_call x1, Pallas kernels, local(): pl.pallas_call(kernel, out_shape=jax.ShapeDtypeStruct((nodes, width), BF1...  52.5 us
    unnamed x1, local copies, waits for them, and re-layouts  1.87 us

profile of v1, /device:TPU:1, one launch (start us, length us, event | category | flops | bytes accessed | tf_op | source)
XLA Modules:
  0.0 54.4 jit_solution(14143875379092781925)
XLA Ops:
  0.0 52.5 %encoder_processor.1 = bf16[256,1024]{1,0:T(8,128)(2,1)} custom-call(s32[12,256]{1,0:T(8,128)} %edge_s.1, s32[64]{0:T(128)} %count_s.1, bf16[4096,128]{1,0:T(8,128)(2,1)} %grid.1, bf16[256,1024]{1,0:T(8,128)(2,1)} %mesh_in.1, f32[96,256]{1,0:T(8,128)} %bitcast.3, f32[2056,256]{1,0:T(8,128)} %bitcast.2, bf16[128,1024]{1,0:T(8,128)(2,1)} %w_embed.1, ...), custom_call_target="tpu_custom_call" | custom-call | tf_op jit(solution)/shard_map/encoder_processor/pallas_call | solution.py:441
  52.5 1.9 %copy.20 = bf16[256,1024]{1,0:T(8,128)(2,1)} copy(bf16[256,1024]{1,0:T(8,128)(2,1)} %encoder_processor.1) | data formatting | bytes 1048576

commit v2 on v1

--- a/solution.py
+++ b/solution.py
@@ -12,7 +12,8 @@
 BF16 = jnp.bfloat16
 LANES = 128
 BLOCK = 16
-CHUNKS = 4
+CHUNKS = 8
+RING = 4
 VMEM_BYTES = 60 * 1024 * 1024
 
 
@@ -35,22 +36,23 @@
 
 
 def kernel(
-    edge_s, count_s, grid, mesh_in, enc_bias, proc_bias, w_embed,
+    count_s, enc_edges, grid, mesh_in, enc_bias, proc_bias, w_embed,
     enc_query, enc_key, enc_value, enc_out,
     proc_query, proc_key, proc_value, proc_out, mlp_gate, mlp_up, mlp_down,
     out,
-    ext, extf, mesh_v, we_v, eq_v, ek_v, ev_v, eo_v, pq_v, pk_v, pv_v, po_v,
-    gate_v, up_v, down_v, eb_v, pb_v, bd, qk, wv, g, u_s, lat, nx, q_s, k_s, v_s,
+    edge_s, ext, extf, mesh_v, we_v, eq_v, ek_v, ev_v, eo_v, pq_v, pk_v, pv_v, po_v,
+    gate_v, up_v, down_v, eb_v, pb_v, bd, qk, vmap, apart, marks, g, u_s, lat, nx, q_s, k_s, v_s,
     hid, part, wo, psend, precv, ob,
     load_sem, gs_sem, gr_sem, fs_sem, fr_sem, xs_sem, xr_sem, ls_sem, lr_sem,
-    hs_sem, hr_sem, ps_sem, pr_sem, os_sem,
+    hs_sem, hr_sem, ks_sem, kr_sem, ps_sem, pr_sem, os_sem,
 ):
     band, core = lax.axis_index("band"), lax.axis_index("head")
     bands = lax.axis_size("band")
     other = 1 - core
-    left = lax.rem(band + bands - 1, bands)
-    right = lax.rem(band + 1, bands)
+    has_left, has_right = band > 0, band < bands - 1
+    left, right = jnp.maximum(band - 1, 0), jnp.minimum(band + 1, bands - 1)
     toward = jnp.where(core == 1, right, left)
+    has_toward = band != toward
     grid_rows = grid.shape[0]
     nodes = mesh_in.shape[0]
     half = nodes // 2
@@ -60,14 +62,22 @@
     pairs = local_heads // 2
     edges = edge_s.shape[0]
 
+    def when(condition, action):
+        pl.when(condition)(action)
+
     def mesh_id(b, h):
         return {"band": b, "head": h}
+
+    def ring_rows(b, start, size):
+        first = lax.rem(b, RING) * grid_rows + start
+        return pl.ds(pl.multiple_of(first, grid_rows // 2 // CHUNKS), size)
 
     own = pl.ds(pl.multiple_of(core * local_width, LANES), local_width)
     theirs = pl.ds(pl.multiple_of(other * local_width, LANES), local_width)
     bias_rows = enc_bias.shape[0]
     sources = [
         (mesh_in, mesh_v),
+        (enc_edges.at[:, pl.ds(pl.multiple_of(core * half, LANES), half)], edge_s),
         (enc_query, eq_v),
         (w_embed, we_v),
         (enc_key, ek_v),
@@ -76,7 +86,7 @@
         (enc_bias.at[:, pl.ds(half, half)], eb_v.at[1, pl.ds(0, bias_rows)]),
         (proc_bias.at[:, pl.ds(0, half)], pb_v.at[0]),
         (proc_bias.at[:, pl.ds(half, half)], pb_v.at[1]),
-        (grid, ext.at[pl.ds(grid_rows, grid_rows)]),
+        (grid, ext.at[ring_rows(band, 0, grid_rows)]),
         (enc_out.at[own], eo_v.at[pl.ds(0, local_width)]),
         (enc_out.at[theirs], eo_v.at[pl.ds(local_width, local_width)]),
         (mlp_gate, gate_v),
@@ -91,20 +101,22 @@
         pltpu.make_async_copy(src, dst, load_sem.at[i]) for i, (src, dst) in enumerate(sources)
     ]
     (
-        l_mesh, l_eq, l_we, l_ek, l_ev, l_eb0, l_eb1, l_pb0, l_pb1, l_grid, l_eo0, l_eo1,
+        l_mesh, l_edge, l_eq, l_we, l_ek, l_ev, l_eb0, l_eb1, l_pb0, l_pb1, l_grid, l_eo0, l_eo1,
         l_gate, l_up, l_pq, l_pk, l_pv, l_down, l_po,
     ) = loads
-    for load in loads[:9]:
+    for load in loads[:10]:
         load.start()
 
     barrier = pltpu.get_barrier_semaphore()
-    for partner in (
-        mesh_id(band, other), mesh_id(left, core), mesh_id(right, core), mesh_id(toward, other)
-    ):
-        pl.semaphore_signal(
-            barrier, inc=1, device_id=partner, device_id_type=pl.DeviceIdType.MESH
-        )
-    pl.semaphore_wait(barrier, 4)
+    def greet(device):
+        pl.semaphore_signal(barrier, inc=1, device_id=device, device_id_type=pl.DeviceIdType.MESH)
+
+    greet(mesh_id(band, other))
+    when(has_left, lambda: greet(mesh_id(left, core)))
+    when(has_right, lambda: greet(mesh_id(right, core)))
+    when(has_toward, lambda: greet(mesh_id(toward, other)))
+    met = 1 + sum(jnp.where(flag, 1, 0) for flag in (has_left, has_right, has_toward))
+    pl.semaphore_wait(barrier, met)
 
     def remote(src, dst, send, recv, device):
         return pltpu.make_async_remote_copy(
@@ -116,25 +128,29 @@
     halo = []
     passed = []
     for k in range(CHUNKS):
-        src_row = pl.multiple_of(core * (grid_rows // 2) + k * piece, piece)
-        far_row = pl.multiple_of(other * (grid_rows // 2) + k * piece, piece)
-        for d, device in ((0, right), (1, left)):
-            start = 2 * grid_rows * d
+        start = core * (grid_rows // 2) + k * piece
+        for d, (target, source) in enumerate(((right, left), (left, right))):
             slot = d * CHUNKS + k
             halo.append(
                 remote(
-                    grid.at[pl.ds(src_row, piece)],
-                    ext.at[pl.ds(pl.multiple_of(start + src_row, piece), piece)],
-                    gs_sem.at[slot], gr_sem.at[slot], mesh_id(device, core),
+                    grid.at[pl.ds(pl.multiple_of(start, piece), piece)],
+                    ext.at[ring_rows(band, start, piece)],
+                    gs_sem.at[slot], gr_sem.at[slot], mesh_id(target, core),
                 )
             )
-            here = ext.at[pl.ds(pl.multiple_of(start + src_row, piece), piece)]
+            here = ext.at[ring_rows(source, start, piece)]
             passed.append(
                 remote(here, here, fs_sem.at[slot], fr_sem.at[slot], mesh_id(band, other))
             )
-    for copy in halo:
-        copy.start()
-    for load in loads[9:]:
+    sides = (has_left, has_right)
+
+    def start_all(copies):
+        for copy in copies:
+            copy.start()
+
+    when(has_right, lambda: start_all(halo[0::2]))
+    when(has_left, lambda: start_all(halo[1::2]))
+    for load in loads[10:]:
         load.start()
 
     padding = eb_v.shape[1] - bias_rows
@@ -148,7 +164,12 @@
     l_ek.wait()
     key_map = nn(we_v[...], ek_v[...]).astype(BF16)
     l_ev.wait()
-    wv[0] = nn(we_v[...], ev_v[...]).astype(BF16)
+    value_map = nn(we_v[...], ev_v[...])
+    low_lanes = iota((LANES, LANES), 1) < HDIM
+    for pair in range(pairs):
+        both = value_map[:, pair * LANES : (pair + 1) * LANES]
+        vmap[pair, 0:LANES, :] = jnp.where(low_lanes, both, 0.0).astype(BF16)
+        vmap[pair, LANES : 2 * LANES, :] = jnp.where(low_lanes, 0.0, both).astype(BF16)
     l_eb0.wait()
     l_eb1.wait()
     low_half = iota((nodes, LANES), 1) < HDIM
@@ -168,7 +189,7 @@
             qk[slot, h, :, LANES : 2 * LANES] = lanes.T.astype(BF16)
     exchange = [
         remote(qk.at[1], qk.at[2], xs_sem.at[0], xr_sem.at[0], mesh_id(band, other)),
-        remote(wv.at[0], wv.at[1], xs_sem.at[1], xr_sem.at[1], mesh_id(band, other)),
+        remote(vmap.at[0:pairs], vmap.at[pairs : 2 * pairs], xs_sem.at[1], xr_sem.at[1], mesh_id(band, other)),
     ]
     for copy in exchange:
         copy.start()
@@ -177,8 +198,8 @@
     span = nodes + 2 * reach
     window = 3 * half
     own_count = count_s[band]
-    lower_count = jnp.where(band > 0, count_s[left], 0)
-    upper_count = jnp.where(band < bands - 1, count_s[right], 0)
+    lower_count = jnp.where(has_left, count_s[left], 0)
+    upper_count = jnp.where(has_right, count_s[right], 0)
     key_slot = iota((1, span), 1)
     before, after = key_slot < reach, key_slot >= reach + nodes
     limit = jnp.where(before, lower_count, jnp.where(after, upper_count, own_count))
@@ -202,79 +223,77 @@
             )
             bd[h, i] = jnp.where(usable, skewed, NEGATIVE)
 
-    def widen(k, d, which):
-        start = pl.multiple_of(
-            2 * grid_rows * d + which * (grid_rows // 2) + k * piece, piece
-        )
-        rows = pl.ds(start, piece)
+    def widen(rows):
         extf[rows, :] = ext[rows, :].astype(F32)
 
+    def arrive(k, d):
+        halo[2 * k + d].wait_recv()
+        passed[2 * k + d].start()
+        widen(ring_rows((left, right)[d], core * (grid_rows // 2) + k * piece, piece))
+
+    def arrive_passed(k, d):
+        passed[2 * k + d].wait_recv()
+        widen(ring_rows((left, right)[d], other * (grid_rows // 2) + k * piece, piece))
+
+    blocks = half // BLOCK
+    block_rows = 16 * BLOCK
+    row = iota((block_rows, block_rows), 0)
+    column = iota((block_rows, block_rows), 1)
+    same = ((row & (BLOCK - 1)) == (column & (BLOCK - 1))) & (column < edges * BLOCK)
+    apart[...] = jnp.where(same, 0.0, NEGATIVE)
+    lane = iota((block_rows, LANES), 1)
+    edge_of_row = iota((block_rows, LANES), 0) >> 4
+    mark = (lane < 48) & ((lane & 15) == edge_of_row)
+    marks[...] = jnp.where(mark, 1.0, 0.0).astype(BF16)
     v_s[...] = jnp.ones(v_s.shape, BF16)
-    g[...] = jnp.zeros(g.shape, F32)
+    for block in range(blocks):
+        unused = slice(block * block_rows + edges * BLOCK, (block + 1) * block_rows)
+        g[unused, :] = jnp.zeros((block_rows - edges * BLOCK, LANES), F32)
+    l_edge.wait()
     l_grid.wait()
+    for h in range(local_heads):
+        window_bias(h)
     for k in range(CHUNKS):
-        for h in range(k * local_heads // CHUNKS, (k + 1) * local_heads // CHUNKS):
-            window_bias(h)
-        own_rows = pl.ds(grid_rows + k * 2 * piece, 2 * piece)
-        extf[own_rows, :] = ext[own_rows, :].astype(F32)
+        widen(ring_rows(band, 2 * k * piece, 2 * piece))
         for d in range(2):
-            halo[2 * k + d].wait_recv()
-            passed[2 * k + d].start()
-        for d in range(2):
-            widen(k, d, core)
+            when(sides[d], lambda k=k, d=d: arrive(k, d))
         if k > 0:
             for d in range(2):
-                passed[2 * (k - 1) + d].wait_recv()
-                widen(k - 1, d, other)
-    for d in range(2):
-        passed[2 * (CHUNKS - 1) + d].wait_recv()
-        widen(CHUNKS - 1, d, other)
-
-    base = (band - 1) * grid_rows
-    blocks = half // BLOCK
-    block_rows = 16 * BLOCK
-
-    def gather(i, carry):
-        block, edge = i // edges, lax.rem(i, edges)
-        for n in range(BLOCK):
-            row = jnp.maximum(edge_s[edge, core * half + block * BLOCK + n] - base, 0)
-            g[pl.ds(block * block_rows + edge * BLOCK + n, 1), :] = extf[pl.ds(row, 1), :]
-        return carry
-
-    lax.fori_loop(0, blocks * edges, gather, 0)
-
+                when(sides[d], lambda k=k, d=d: arrive_passed(k - 1, d))
     for copy in exchange:
         copy.wait()
-    lane = iota((block_rows, LANES), 1)
-    edge_of_row = iota((block_rows, LANES), 0) // BLOCK
-    marks = (lane < 48) & (lax.rem(lane, 16) == edge_of_row)
-    marks = marks.astype(F32).astype(BF16)
+    for d in range(2):
+        when(sides[d], lambda d=d: arrive_passed(CHUNKS - 1, d))
+
+    def gather(block):
+        for edge in range(edges):
+            found = []
+            for n in range(BLOCK):
+                row = edge_s[edge, block * BLOCK + n] & (RING * grid_rows - 1)
+                found.append(extf[pl.ds(row, 1), :])
+            for n in range(BLOCK):
+                g[pl.ds(block * block_rows + edge * BLOCK + n, 1), :] = found[n]
+
     ones = jnp.ones((block_rows, LANES), BF16)
-    row = iota((block_rows, block_rows), 0)
-    column = iota((block_rows, block_rows), 1)
-    same = (lax.rem(row, BLOCK) == lax.rem(column, BLOCK)) & (column < edges * BLOCK)
+    gather(0)
     for block in range(blocks):
+        if block + 1 < blocks:
+            gather(block + 1)
         rows = slice(block * BLOCK, (block + 1) * BLOCK)
         near = g[block * block_rows : (block + 1) * block_rows, :].astype(BF16)
         asked = jnp.concatenate(
             [qk[s, :, rows, :].reshape(local_heads * BLOCK, 2 * LANES) for s in (0, 2)], 0
         )
-        scores = jnp.where(same, nt(asked, jnp.concatenate([near, marks], 1)), NEGATIVE)
+        scores = nt(asked, jnp.concatenate([near, marks[...]], 1)) + apart[...]
         peak = jnp.max(scores, 1, keepdims=True)
         weights = jnp.exp(scores - peak).astype(BF16)
         mixed = nn(weights, jnp.concatenate([near, ones], 1))
         mixed = (mixed[:, :LANES] / mixed[:, LANES:]).astype(BF16)
         for h in range(2 * local_heads):
             u_s[rows, h * LANES : (h + 1) * LANES] = mixed[h * BLOCK : (h + 1) * BLOCK]
-    low_lanes = iota((LANES, LANES), 1) < HDIM
     attended = []
     for pair in range(2 * pairs):
-        value_map = wv[pair // pairs, :, pair % pairs * LANES : (pair % pairs + 1) * LANES]
-        value_map = value_map.astype(F32)
-        value_map = jnp.concatenate(
-            [jnp.where(low_lanes, value_map, 0.0), jnp.where(low_lanes, 0.0, value_map)], 0
-        ).astype(BF16)
-        attended.append(nn(u_s[:, pair * 2 * LANES : (pair + 1) * 2 * LANES], value_map))
+        attended.append(nn(u_s[:, pair * 2 * LANES : (pair + 1) * 2 * LANES], vmap[pair]))
     attended = jnp.concatenate(attended, 1).astype(BF16)
     l_eo0.wait()
     l_eo1.wait()
@@ -284,13 +303,40 @@
     to_sibling = remote(lat.at[core], lat.at[core], ls_sem.at[0], lr_sem.at[0], mesh_id(band, other))
     to_sibling.start()
     nx[1 + core] = normalize(latent.astype(F32))
-    slot = 3 * other
+
+    quarter = half // 2
+
+    def part_of(slot, which):
+        return nx.at[slot, pl.ds(pl.multiple_of(which * quarter, quarter), quarter)]
+
     sends = [
-        remote(nx.at[1 + core], nx.at[slot], hs_sem.at[0], hr_sem.at[slot], mesh_id(toward, core)),
-        remote(nx.at[1 + core], nx.at[slot], hs_sem.at[1], hr_sem.at[slot], mesh_id(toward, other)),
+        remote(
+            part_of(1 + core, which), part_of(3 * other, which),
+            hs_sem.at[i], hr_sem.at[3 * other], mesh_id(toward, which),
+        )
+        for i, which in enumerate((core, other))
     ]
-    for copy in sends:
-        copy.start()
+    when(has_toward, lambda: start_all(sends))
+    handed = [
+        remote(
+            part_of(s, core), part_of(s, core),
+            ks_sem.at[d], kr_sem.at[d], mesh_id(band, other),
+        )
+        for d, s in enumerate((0, 3))
+    ]
+
+    def hand(d):
+        s = 3 * d
+        remote(
+            part_of(s, core), part_of(s, core), hs_sem.at[0], hr_sem.at[s], mesh_id(toward, core)
+        ).wait_recv()
+        handed[d].start()
+
+    def clear(s):
+        nx[s] = jnp.zeros((half, width), BF16)
+
+    when(jnp.logical_not(has_left), lambda: clear(0))
+    when(jnp.logical_not(has_right), lambda: clear(3))
     to_sibling.wait_recv()
     nx[2 - core] = normalize(lat[other].astype(F32))
     normed = nx[1:3].reshape(nodes, width)
@@ -303,6 +349,8 @@
         gated = nn(normed, gate_v[:, columns])
         raised = nn(normed, up_v[:, columns])
         hid[:, columns] = (0.5 * gated * (1.0 + jnp.tanh(0.5 * gated)) * raised).astype(BF16)
+    for d in range(2):
+        when(sides[d], lambda d=d: hand(d))
     l_pq.wait()
     win_query = nn(normed, pq_v[...]).astype(BF16)
     q_s[...] = (win_query.astype(F32) * HDIM**-0.5).astype(BF16)
@@ -323,11 +371,17 @@
         columns = slice(ch * step, (ch + 1) * step)
         part[:, columns] = nn(hid[...], down_v[:, columns])
 
-    for s, at in ((0, 0), (3, reach + nodes)):
-        remote(
-            nx.at[s], nx.at[s], hs_sem.at[0], hr_sem.at[s], mesh_id(toward, core)
-        ).wait_recv()
-        keys_values(slice(at, at + reach), nx[s])
+    for d in range(2):
+        when(sides[d], handed[d].wait_recv)
+    outer = jnp.concatenate([nx[0], nx[3]], 0)
+    outer_keys = nn(outer, pk_v[...]).astype(BF16)
+    outer_values = nn(outer, pv_v[...]).astype(BF16)
+    for s, rows in ((0, slice(0, reach)), (1, slice(reach + nodes, span))):
+        k_s[rows, :] = outer_keys[s * reach : (s + 1) * reach]
+        for pair in range(pairs):
+            v_s[rows, pair * 2 * LANES : pair * 2 * LANES + LANES] = outer_values[
+                s * reach : (s + 1) * reach, pair * LANES : (pair + 1) * LANES
+            ]
 
     l_po.wait()
     results = []
@@ -366,8 +420,15 @@
         store = pltpu.make_async_copy(ob.at[i], out.at[pl.ds(i * half, half)], os_sem.at[i])
         store.start()
         stores.append(store)
-    for copy in halo + passed + [to_sibling] + sends + results:
-        copy.wait_send()
+
+    def sent(copies):
+        for copy in copies:
+            copy.wait_send()
+
+    when(has_right, lambda: sent(halo[0::2] + passed[1::2] + handed[1:]))
+    when(has_left, lambda: sent(halo[1::2] + passed[0::2] + handed[:1]))
+    when(has_toward, lambda: sent(sends))
+    sent([to_sibling] + results)
     for store in stores:
         store.wait()
 
@@ -390,8 +451,9 @@
     dma = pltpu.SemaphoreType.DMA
     vmem = pltpu.VMEM
     scratch = [
-        vmem((3 * grid_rows, channels), BF16),
-        vmem((3 * grid_rows, channels), F32),
+        pltpu.SMEM((edges, half), jnp.int32),
+        vmem((RING * grid_rows, channels), BF16),
+        vmem((RING * grid_rows, channels), F32),
         vmem((nodes, width), BF16),
         vmem((channels, width), BF16),
         vmem((width, local_width), BF16),
@@ -409,7 +471,9 @@
         vmem((2, proc_bias.shape[0], half), F32),
         vmem((heads, 2, half, 3 * half), F32),
         vmem((3, heads, half, 2 * LANES), BF16),
-        vmem((2, channels, local_width), BF16),
+        vmem((heads, 2 * LANES, LANES), BF16),
+        vmem((16 * BLOCK, 16 * BLOCK), F32),
+        vmem((16 * BLOCK, LANES), BF16),
         vmem((half * 16, channels), F32),
         vmem((half, 2 * heads * channels), BF16),
         vmem((2, half, width), BF16),
@@ -423,7 +487,7 @@
         vmem((2, half, width), BF16),
         vmem((2, half, width), BF16),
         vmem((2, half, width), BF16),
-        dma((19,)),
+        dma((20,)),
         dma((2 * CHUNKS,)),
         dma((2 * CHUNKS,)),
         dma((2 * CHUNKS,)),
@@ -437,11 +501,13 @@
         dma((2,)),
         dma((2,)),
         dma((2,)),
+        dma((2,)),
+        dma((2,)),
     ]
     return pl.pallas_call(
         kernel,
         out_shape=jax.ShapeDtypeStruct((nodes, width), BF16),
-        in_specs=[in_scalar, in_scalar] + [anywhere] * 16,
+        in_specs=[in_scalar] + [anywhere] * 17,
         out_specs=anywhere,
         scratch_shapes=scratch,
         compiler_params=pltpu.CompilerParams(
@@ -449,7 +515,7 @@
         ),
         name="encoder_processor",
     )(
-        enc_edges, counts, grid_in, mesh_in, enc_bias, proc_bias, w_embed, enc_query, enc_key,
+        counts, enc_edges, grid_in, mesh_in, enc_bias, proc_bias, w_embed, enc_query, enc_key,
         enc_value, enc_out, proc_query, proc_key, proc_value, proc_out, mlp_gate, mlp_up, mlp_down,
     )
 

time: 54.6 us -> 42.7 us (0.78)
  the two profiles are of different devices: /device:TPU:1 before, /device:TPU:97 now
where the time goes in v2:
time: 42.7 us; the launch traced here: 42.5 us
  Pallas kernels  40.6 us (95%)
  local copies, waits for them, and re-layouts  1.87 us (4%)
    pallas_call x1, Pallas kernels, local(): pl.pallas_call(kernel, out_shape=jax.ShapeDtypeStruct((nodes, width), BF1...  40.6 us
    unnamed x1, local copies, waits for them, and re-layouts  1.87 us

profile of v2, /device:TPU:97, one launch (start us, length us, event | category | flops | bytes accessed | tf_op | source)
XLA Modules:
  0.0 42.5 jit_solution(173254811149382681)
XLA Ops:
  0.0 40.6 %encoder_processor.1 = bf16[256,1024]{1,0:T(8,128)(2,1)} custom-call(s32[64]{0:T(128)} %count_s.1, s32[12,256]{1,0:T(8,128)} %enc_edges.1, bf16[4096,128]{1,0:T(8,128)(2,1)} %grid.1, bf16[256,1024]{1,0:T(8,128)(2,1)} %mesh_in.1, f32[96,256]{1,0:T(8,128)} %bitcast.3, f32[2056,256]{1,0:T(8,128)} %bitcast.2, bf16[128,1024]{1,0:T(8,128)(2,1)} %w_embed.1, ...), custom_call_target="tpu_custom_call" | custom-call | tf_op jit(solution)/shard_map/encoder_processor/pallas_call | solution.py:507
  40.6 1.9 %copy.20 = bf16[256,1024]{1,0:T(8,128)(2,1)} copy(bf16[256,1024]{1,0:T(8,128)(2,1)} %encoder_processor.1) | data formatting | bytes 1048576

commit v3 on v2

--- a/solution.py
+++ b/solution.py
@@ -42,9 +42,9 @@
     out,
     edge_s, ext, extf, mesh_v, we_v, eq_v, ek_v, ev_v, eo_v, pq_v, pk_v, pv_v, po_v,
     gate_v, up_v, down_v, eb_v, pb_v, bd, qk, vmap, apart, marks, g, u_s, lat, nx, q_s, k_s, v_s,
-    hid, part, wo, psend, precv, ob,
+    hid, part, wo, psend, precv,
     load_sem, gs_sem, gr_sem, fs_sem, fr_sem, xs_sem, xr_sem, ls_sem, lr_sem,
-    hs_sem, hr_sem, ks_sem, kr_sem, ps_sem, pr_sem, os_sem,
+    hs_sem, hr_sem, ks_sem, kr_sem, ps_sem, pr_sem,
 ):
     band, core = lax.axis_index("band"), lax.axis_index("head")
     bands = lax.axis_size("band")
@@ -221,7 +221,7 @@
             usable = in_window & (
                 (live[:, i * half : i * half + window] > 0) | (offset == reach)
             )
-            bd[h, i] = jnp.where(usable, skewed, NEGATIVE)
+            bd[h // 2, i, h % 2 * half : (h % 2 + 1) * half] = jnp.where(usable, skewed, NEGATIVE)
 
     def widen(rows):
         extf[rows, :] = ext[rows, :].astype(F32)
@@ -341,85 +341,75 @@
     nx[2 - core] = normalize(lat[other].astype(F32))
     normed = nx[1:3].reshape(nodes, width)
 
+    l_pq.wait()
+    win_query = nn(normed, pq_v[...]).astype(BF16)
+    win_query = win_query.astype(F32) * HDIM**-0.5
+    first_head = iota((half, LANES), 1) < HDIM
+    for i in range(2):
+        for pair in range(pairs):
+            both = win_query[i * half : (i + 1) * half, pair * LANES : (pair + 1) * LANES]
+            q_s[i, pair, 0:half, :] = jnp.where(first_head, both, 0.0).astype(BF16)
+            q_s[i, pair, half:nodes, :] = jnp.where(first_head, 0.0, both).astype(BF16)
+    l_pk.wait()
+    l_pv.wait()
+
+    def keys_values(source, places):
+        keys = nn(source, pk_v[...]).astype(BF16)
+        values = nn(source, pv_v[...]).astype(BF16)
+        for n, rows in enumerate(places):
+            have = slice(n * half, (n + 1) * half)
+            k_s[rows, :] = keys[have]
+            for pair in range(pairs):
+                v_s[rows, pair * 2 * LANES : pair * 2 * LANES + LANES] = values[
+                    have, pair * LANES : (pair + 1) * LANES
+                ]
+
+    keys_values(normed, (slice(half, 2 * half), slice(2 * half, 3 * half)))
     l_gate.wait()
     l_up.wait()
     step = 512
-    for ch in range(gate_v.shape[1] // step):
+    steps = gate_v.shape[1] // step
+    for ch in range(steps):
+        if ch == steps // 2:
+            for d in range(2):
+                when(sides[d], lambda d=d: hand(d))
         columns = slice(ch * step, (ch + 1) * step)
         gated = nn(normed, gate_v[:, columns])
         raised = nn(normed, up_v[:, columns])
         hid[:, columns] = (0.5 * gated * (1.0 + jnp.tanh(0.5 * gated)) * raised).astype(BF16)
-    for d in range(2):
-        when(sides[d], lambda d=d: hand(d))
-    l_pq.wait()
-    win_query = nn(normed, pq_v[...]).astype(BF16)
-    q_s[...] = (win_query.astype(F32) * HDIM**-0.5).astype(BF16)
-    l_pk.wait()
-    l_pv.wait()
-
-    def keys_values(rows, source):
-        k_s[rows, :] = nn(source, pk_v[...]).astype(BF16)
-        values = nn(source, pv_v[...]).astype(BF16)
-        for pair in range(pairs):
-            v_s[rows, pair * 2 * LANES : pair * 2 * LANES + LANES] = values[
-                :, pair * LANES : (pair + 1) * LANES
-            ]
-
-    keys_values(slice(reach, reach + nodes), normed)
     l_down.wait()
-    for ch in range(width // step):
-        columns = slice(ch * step, (ch + 1) * step)
-        part[:, columns] = nn(hid[...], down_v[:, columns])
-
+    l_po.wait()
     for d in range(2):
         when(sides[d], handed[d].wait_recv)
     outer = jnp.concatenate([nx[0], nx[3]], 0)
-    outer_keys = nn(outer, pk_v[...]).astype(BF16)
-    outer_values = nn(outer, pv_v[...]).astype(BF16)
-    for s, rows in ((0, slice(0, reach)), (1, slice(reach + nodes, span))):
-        k_s[rows, :] = outer_keys[s * reach : (s + 1) * reach]
-        for pair in range(pairs):
-            v_s[rows, pair * 2 * LANES : pair * 2 * LANES + LANES] = outer_values[
-                s * reach : (s + 1) * reach, pair * LANES : (pair + 1) * LANES
-            ]
-
-    l_po.wait()
+    keys_values(outer, (slice(0, half), slice(3 * half, 4 * half)))
     results = []
-    first_head = iota((half, LANES), 1) < HDIM
     for i in range(2):
         rows = slice(i * half, (i + 1) * half)
         seen = slice(i * half, i * half + window)
         for pair in range(pairs):
+            if i == 0:
+                columns = slice(pair * width // pairs, (pair + 1) * width // pairs)
+                part[:, columns] = nn(hid[...], down_v[:, columns])
             columns = slice(pair * LANES, (pair + 1) * LANES)
-            asked = q_s[rows, columns].astype(F32)
-            keys = k_s[seen, columns]
-            values = v_s[seen, pair * 2 * LANES : (pair + 1) * 2 * LANES]
-            outs = []
-            for h in range(2):
-                keep = first_head if h == 0 else jnp.logical_not(first_head)
-                masked = jnp.where(keep, asked, 0.0).astype(BF16)
-                scores = nt(masked, keys) + bd[pair * 2 + h, i]
-                peak = jnp.max(scores, 1, keepdims=True)
-                weights = jnp.exp(scores - peak).astype(BF16)
-                mixed = nn(weights, values)
-                outs.append(mixed[:, :LANES] / mixed[:, LANES:])
-            wo[rows, columns] = jnp.where(first_head, outs[0], outs[1]).astype(BF16)
+            scores = nt(q_s[i, pair], k_s[seen, columns]) + bd[pair, i]
+            peak = jnp.max(scores, 1, keepdims=True)
+            weights = jnp.exp(scores - peak).astype(BF16)
+            mixed = nn(weights, v_s[seen, pair * 2 * LANES : (pair + 1) * 2 * LANES])
+            mixed = mixed[:, :LANES] / mixed[:, LANES:]
+            wo[rows, columns] = jnp.where(first_head, mixed[:half], mixed[half:]).astype(BF16)
         psend[i] = (part[rows, :] + nn(wo[rows, :], po_v[...])).astype(BF16)
         result = remote(
             psend.at[i], precv.at[i], ps_sem.at[i], pr_sem.at[i], mesh_id(band, other)
         )
         result.start()
         results.append(result)
-    stores = []
     for i in range(2):
         results[i].wait_recv()
         summed = psend[i].astype(F32) + precv[i].astype(F32)
         node = iota((half, width), 0) + i * half
         scale = (node < own_count).astype(F32)
-        ob[i] = ((lat[i].astype(F32) + summed) * scale).astype(BF16)
-        store = pltpu.make_async_copy(ob.at[i], out.at[pl.ds(i * half, half)], os_sem.at[i])
-        store.start()
-        stores.append(store)
+        out[i * half : (i + 1) * half, :] = ((lat[i].astype(F32) + summed) * scale).astype(BF16)
 
     def sent(copies):
         for copy in copies:
@@ -429,8 +419,6 @@
     when(has_left, lambda: sent(halo[1::2] + passed[0::2] + handed[:1]))
     when(has_toward, lambda: sent(sends))
     sent([to_sibling] + results)
-    for store in stores:
-        store.wait()
 
 
 def local(
@@ -469,7 +457,7 @@
         vmem((hidden, width), BF16),
         vmem((2, 16 * heads, half), F32),
         vmem((2, proc_bias.shape[0], half), F32),
-        vmem((heads, 2, half, 3 * half), F32),
+        vmem((heads // 2, 2, 2 * half, 3 * half), F32),
         vmem((3, heads, half, 2 * LANES), BF16),
         vmem((heads, 2 * LANES, LANES), BF16),
         vmem((16 * BLOCK, 16 * BLOCK), F32),
@@ -478,7 +466,7 @@
         vmem((half, 2 * heads * channels), BF16),
         vmem((2, half, width), BF16),
         vmem((4, half, width), BF16),
-        vmem((nodes, local_width), BF16),
+        vmem((2, heads // 2, nodes, LANES), BF16),
         vmem((2 * nodes, local_width), BF16),
         vmem((2 * nodes, 2 * local_width), BF16),
         vmem((nodes, hidden), BF16),
@@ -486,7 +474,6 @@
         vmem((nodes, local_width), BF16),
         vmem((2, half, width), BF16),
         vmem((2, half, width), BF16),
-        vmem((2, half, width), BF16),
         dma((20,)),
         dma((2 * CHUNKS,)),
         dma((2 * CHUNKS,)),
@@ -502,13 +489,12 @@
         dma((2,)),
         dma((2,)),
         dma((2,)),
-        dma((2,)),
     ]
     return pl.pallas_call(
         kernel,
-        out_shape=jax.ShapeDtypeStruct((nodes, width), BF16),
+        out_shape=pltpu.VMEM((nodes, width), BF16),
         in_specs=[in_scalar] + [anywhere] * 17,
-        out_specs=anywhere,
+        out_specs=pl.BlockSpec(memory_space=pltpu.VMEM),
         scratch_shapes=scratch,
         compiler_params=pltpu.CompilerParams(
             collective_id=0, has_side_effects=True, vmem_limit_bytes=VMEM_BYTES

time: 42.7 us -> 41.1 us (0.963)
  local copies, waits for them, and re-layouts: 1.87 us -> 0.8 us
    unnamed x1, local copies, waits for them, and re-layouts: 1.87 us -> 0.8 us
where the time goes in v3:
time: 41.1 us; the launch traced here: 41 us
  Pallas kernels  40.2 us (98%)
  local copies, waits for them, and re-layouts  0.8 us (2%)
    pallas_call x1, Pallas kernels, local(): pl.pallas_call(kernel, out_shape=pltpu.VMEM((nodes, width), BF16), in_spe...  40.2 us

profile of v3, /device:TPU:97, one launch (start us, length us, event | category | flops | bytes accessed | tf_op | source)
XLA Modules:
  0.0 41.0 jit_solution(10693070152085263288)
XLA Ops:
  0.0 40.2 %encoder_processor.1 = bf16[256,1024]{1,0:T(8,128)(2,1)S(1)} custom-call(s32[64]{0:T(128)} %count_s.1, s32[12,256]{1,0:T(8,128)} %enc_edges.1, bf16[4096,128]{1,0:T(8,128)(2,1)} %grid.1, bf16[256,1024]{1,0:T(8,128)(2,1)} %mesh_in.1, f32[96,256]{1,0:T(8,128)} %bitcast.3, f32[2056,256]{1,0:T(8,128)} %bitcast.2, bf16[128,1024]{1,0:T(8,128)(2,1)} %w_embed.1, ...), custom_call_target="tpu_custom_call" | custom-call | tf_op jit(solution)/shard_map/encoder_processor/pallas_call | solution.py:493
  40.2 0.8 %copy.20 = bf16[256,1024]{1,0:T(8,128)(2,1)} copy(bf16[256,1024]{1,0:T(8,128)(2,1)S(1)} %encoder_processor.1) | data formatting | bytes 1048576

commit v4 on v3

--- a/solution.py
+++ b/solution.py
@@ -42,8 +42,8 @@
     out,
     edge_s, ext, extf, mesh_v, we_v, eq_v, ek_v, ev_v, eo_v, pq_v, pk_v, pv_v, po_v,
     gate_v, up_v, down_v, eb_v, pb_v, bd, qk, vmap, apart, marks, g, u_s, lat, nx, q_s, k_s, v_s,
-    hid, part, wo, psend, precv,
-    load_sem, gs_sem, gr_sem, fs_sem, fr_sem, xs_sem, xr_sem, ls_sem, lr_sem,
+    hid, part, peaks, sums, wo, psend, precv,
+    load_sem, gs_sem, gr_sem, fs_sem, fr_sem, ds_sem, dr_sem, xs_sem, xr_sem, ls_sem, lr_sem,
     hs_sem, hr_sem, ks_sem, kr_sem, ps_sem, pr_sem,
 ):
     band, core = lax.axis_index("band"), lax.axis_index("head")
@@ -70,7 +70,7 @@
 
     def ring_rows(b, start, size):
         first = lax.rem(b, RING) * grid_rows + start
-        return pl.ds(pl.multiple_of(first, grid_rows // 2 // CHUNKS), size)
+        return pl.ds(pl.multiple_of(first, LANES), size)
 
     own = pl.ds(pl.multiple_of(core * local_width, LANES), local_width)
     theirs = pl.ds(pl.multiple_of(other * local_width, LANES), local_width)
@@ -112,11 +112,14 @@
         pl.semaphore_signal(barrier, inc=1, device_id=device, device_id_type=pl.DeviceIdType.MESH)
 
     greet(mesh_id(band, other))
-    when(has_left, lambda: greet(mesh_id(left, core)))
-    when(has_right, lambda: greet(mesh_id(right, core)))
-    when(has_toward, lambda: greet(mesh_id(toward, other)))
-    met = 1 + sum(jnp.where(flag, 1, 0) for flag in (has_left, has_right, has_toward))
-    pl.semaphore_wait(barrier, met)
+
+    def greet_band(b):
+        greet(mesh_id(b, core))
+        greet(mesh_id(b, other))
+
+    when(has_left, lambda: greet_band(left))
+    when(has_right, lambda: greet_band(right))
+    pl.semaphore_wait(barrier, 1 + jnp.where(has_left, 2, 0) + jnp.where(has_right, 2, 0))
 
     def remote(src, dst, send, recv, device):
         return pltpu.make_async_remote_copy(
@@ -125,31 +128,54 @@
         )
 
     piece = grid_rows // 2 // CHUNKS
+    last_piece = piece // 2
+    sizes = [piece] * (CHUNKS - 1) + [piece - last_piece]
     halo = []
     passed = []
-    for k in range(CHUNKS):
+    direct = []
+    landing = []
+    for k, size in enumerate(sizes):
         start = core * (grid_rows // 2) + k * piece
         for d, (target, source) in enumerate(((right, left), (left, right))):
             slot = d * CHUNKS + k
             halo.append(
                 remote(
-                    grid.at[pl.ds(pl.multiple_of(start, piece), piece)],
-                    ext.at[ring_rows(band, start, piece)],
+                    grid.at[pl.ds(pl.multiple_of(start, LANES), size)],
+                    ext.at[ring_rows(band, start, size)],
                     gs_sem.at[slot], gr_sem.at[slot], mesh_id(target, core),
                 )
             )
-            here = ext.at[ring_rows(source, start, piece)]
+            here = ext.at[ring_rows(source, start, size)]
             passed.append(
                 remote(here, here, fs_sem.at[slot], fr_sem.at[slot], mesh_id(band, other))
             )
+
+    def direct_start(which):
+        return which * (grid_rows // 2) + grid_rows // 2 - last_piece
+
+    for n, peer in enumerate((core, other)):
+        for d, (target, source) in enumerate(((right, left), (left, right))):
+            mine = pl.ds(pl.multiple_of(direct_start(core), LANES), last_piece)
+            direct.append(
+                remote(
+                    grid.at[mine], ext.at[ring_rows(band, direct_start(core), last_piece)],
+                    ds_sem.at[2 * n + d], dr_sem.at[2 * n + d], mesh_id(target, peer),
+                )
+            )
+            here = ext.at[ring_rows(source, direct_start(peer), last_piece)]
+            landing.append(
+                remote(
+                    here, here, ds_sem.at[2 * n + d], dr_sem.at[2 * n + d], mesh_id(target, peer)
+                )
+            )
     sides = (has_left, has_right)
 
     def start_all(copies):
         for copy in copies:
             copy.start()
 
-    when(has_right, lambda: start_all(halo[0::2]))
-    when(has_left, lambda: start_all(halo[1::2]))
+    when(has_right, lambda: start_all(halo[0::2] + direct[0::2]))
+    when(has_left, lambda: start_all(halo[1::2] + direct[1::2]))
     for load in loads[10:]:
         load.start()
 
@@ -229,11 +255,16 @@
     def arrive(k, d):
         halo[2 * k + d].wait_recv()
         passed[2 * k + d].start()
-        widen(ring_rows((left, right)[d], core * (grid_rows // 2) + k * piece, piece))
+        widen(ring_rows((left, right)[d], core * (grid_rows // 2) + k * piece, sizes[k]))
 
     def arrive_passed(k, d):
         passed[2 * k + d].wait_recv()
-        widen(ring_rows((left, right)[d], other * (grid_rows // 2) + k * piece, piece))
+        widen(ring_rows((left, right)[d], other * (grid_rows // 2) + k * piece, sizes[k]))
+
+    def arrive_direct(d):
+        for n, peer in enumerate((core, other)):
+            landing[2 * n + d].wait_recv()
+            widen(ring_rows((left, right)[d], direct_start(peer), last_piece))
 
     blocks = half // BLOCK
     block_rows = 16 * BLOCK
@@ -262,6 +293,8 @@
                 when(sides[d], lambda k=k, d=d: arrive_passed(k - 1, d))
     for copy in exchange:
         copy.wait()
+    for d in range(2):
+        when(sides[d], lambda d=d: arrive_direct(d))
     for d in range(2):
         when(sides[d], lambda d=d: arrive_passed(CHUNKS - 1, d))
 
@@ -304,15 +337,23 @@
     to_sibling.start()
     nx[1 + core] = normalize(latent.astype(F32))
 
-    quarter = half // 2
+    third = half * 3 // 8
+    tail = pl.ds(2 * third, half - 2 * third)
 
     def part_of(slot, which):
-        return nx.at[slot, pl.ds(pl.multiple_of(which * quarter, quarter), quarter)]
+        return nx.at[slot, pl.ds(pl.multiple_of(which * third, 16), third)]
 
     sends = [
         remote(
             part_of(1 + core, which), part_of(3 * other, which),
-            hs_sem.at[i], hr_sem.at[3 * other], mesh_id(toward, which),
+            hs_sem.at[i], hr_sem.at[2 * other], mesh_id(toward, which),
+        )
+        for i, which in enumerate((core, other))
+    ]
+    sends += [
+        remote(
+            nx.at[1 + core, tail], nx.at[3 * other, tail],
+            hs_sem.at[2 + i], hr_sem.at[2 * other + 1], mesh_id(toward, which),
         )
         for i, which in enumerate((core, other))
     ]
@@ -328,9 +369,18 @@
     def hand(d):
         s = 3 * d
         remote(
-            part_of(s, core), part_of(s, core), hs_sem.at[0], hr_sem.at[s], mesh_id(toward, core)
+            part_of(s, core), part_of(s, core),
+            hs_sem.at[0], hr_sem.at[2 * d], mesh_id(toward, core),
         ).wait_recv()
         handed[d].start()
+
+    def all_here(d):
+        s = 3 * d
+        remote(
+            nx.at[s, tail], nx.at[s, tail],
+            hs_sem.at[2], hr_sem.at[2 * d + 1], mesh_id(toward, core),
+        ).wait_recv()
+        handed[d].wait_recv()
 
     def clear(s):
         nx[s] = jnp.zeros((half, width), BF16)
@@ -370,41 +420,54 @@
     step = 512
     steps = gate_v.shape[1] // step
     for ch in range(steps):
-        if ch == steps // 2:
-            for d in range(2):
-                when(sides[d], lambda d=d: hand(d))
         columns = slice(ch * step, (ch + 1) * step)
         gated = nn(normed, gate_v[:, columns])
         raised = nn(normed, up_v[:, columns])
         hid[:, columns] = (0.5 * gated * (1.0 + jnp.tanh(0.5 * gated)) * raised).astype(BF16)
     l_down.wait()
     l_po.wait()
-    for d in range(2):
-        when(sides[d], handed[d].wait_recv)
-    outer = jnp.concatenate([nx[0], nx[3]], 0)
-    keys_values(outer, (slice(0, half), slice(3 * half, 4 * half)))
-    results = []
-    for i in range(2):
-        rows = slice(i * half, (i + 1) * half)
-        seen = slice(i * half, i * half + window)
+    own_keys = slice(half, 3 * half)
+    for i in (1, 0):
+        held = slice((1 - i) * half, (3 - i) * half)
         for pair in range(pairs):
-            if i == 0:
-                columns = slice(pair * width // pairs, (pair + 1) * width // pairs)
+            if pair % 2 == 0:
+                at = ((1 - i) * pairs + pair) // 2 * width // pairs
+                columns = slice(at, at + width // pairs)
                 part[:, columns] = nn(hid[...], down_v[:, columns])
             columns = slice(pair * LANES, (pair + 1) * LANES)
-            scores = nt(q_s[i, pair], k_s[seen, columns]) + bd[pair, i]
+            scores = nt(q_s[i, pair], k_s[own_keys, columns]) + bd[pair, i, :, held]
             peak = jnp.max(scores, 1, keepdims=True)
             weights = jnp.exp(scores - peak).astype(BF16)
+            peaks[i, pair] = jnp.broadcast_to(peak, (nodes, LANES))
+            sums[i, pair] = nn(weights, v_s[own_keys, pair * 2 * LANES : (pair + 1) * 2 * LANES])
+    when(has_right, lambda: hand(1))
+    when(has_left, lambda: hand(0))
+    results = [None, None]
+    for i in (1, 0):
+        when(sides[i], lambda: all_here(i))
+        rows = slice(i * half, (i + 1) * half)
+        seen = slice(3 * i * half, (3 * i + 1) * half)
+        held = slice(2 * i * half, (2 * i + 1) * half)
+        keys_values(nx[3 * i], (seen,))
+        for pair in range(pairs):
+            columns = slice(pair * LANES, (pair + 1) * LANES)
+            scores = nt(q_s[i, pair], k_s[seen, columns]) + bd[pair, i, :, held]
+            before = peaks[i, pair]
+            peak = jnp.maximum(before, jnp.max(scores, 1, keepdims=True))
+            weights = jnp.exp(scores - peak).astype(BF16)
             mixed = nn(weights, v_s[seen, pair * 2 * LANES : (pair + 1) * 2 * LANES])
-            mixed = mixed[:, :LANES] / mixed[:, LANES:]
+            shrink = jnp.exp(before - peak)
+            upper = sums[i, pair, :, 0:LANES] * shrink + mixed[:, :LANES]
+            lower = sums[i, pair, :, LANES : 2 * LANES] * shrink + mixed[:, LANES:]
+            mixed = upper / lower
             wo[rows, columns] = jnp.where(first_head, mixed[:half], mixed[half:]).astype(BF16)
         psend[i] = (part[rows, :] + nn(wo[rows, :], po_v[...])).astype(BF16)
         result = remote(
             psend.at[i], precv.at[i], ps_sem.at[i], pr_sem.at[i], mesh_id(band, other)
         )
         result.start()
-        results.append(result)
-    for i in range(2):
+        results[i] = result
+    for i in (1, 0):
         results[i].wait_recv()
         summed = psend[i].astype(F32) + precv[i].astype(F32)
         node = iota((half, width), 0) + i * half
@@ -415,8 +478,8 @@
         for copy in copies:
             copy.wait_send()
 
-    when(has_right, lambda: sent(halo[0::2] + passed[1::2] + handed[1:]))
-    when(has_left, lambda: sent(halo[1::2] + passed[0::2] + handed[:1]))
+    when(has_right, lambda: sent(halo[0::2] + direct[0::2] + passed[1::2] + handed[1:]))
+    when(has_left, lambda: sent(halo[1::2] + direct[1::2] + passed[0::2] + handed[:1]))
     when(has_toward, lambda: sent(sends))
     sent([to_sibling] + results)
 
@@ -471,6 +534,8 @@
         vmem((2 * nodes, 2 * local_width), BF16),
         vmem((nodes, hidden), BF16),
         vmem((nodes, width), F32),
+        vmem((2, heads // 2, nodes, LANES), F32),
+        vmem((2, heads // 2, nodes, 2 * LANES), F32),
         vmem((nodes, local_width), BF16),
         vmem((2, half, width), BF16),
         vmem((2, half, width), BF16),
@@ -479,11 +544,13 @@
         dma((2 * CHUNKS,)),
         dma((2 * CHUNKS,)),
         dma((2 * CHUNKS,)),
+        dma((4,)),
+        dma((4,)),
         dma((2,)),
         dma((2,)),
         dma((1,)),
         dma((1,)),
-        dma((2,)),
+        dma((4,)),
         dma((4,)),
         dma((2,)),
         dma((2,)),

time: 41.1 us -> 37.9 us (0.922)
  Pallas kernels: 40.2 us -> 37 us
    pallas_call x1, Pallas kernels: 40.2 us -> 37 us  [local(): pl.pallas_call(kernel, out_shape=pltpu.VMEM((nodes, width), BF16), in_spe...]
where the time goes in v4:
time: 37.9 us; the launch traced here: 37.8 us
  Pallas kernels  37 us (98%)
  local copies, waits for them, and re-layouts  0.8 us (2%)
    pallas_call x1, Pallas kernels, local(): pl.pallas_call(kernel, out_shape=pltpu.VMEM((nodes, width), BF16), in_spe...  37 us
    unnamed x1, local copies, waits for them, and re-layouts  0.8 us

profile of v4, /device:TPU:97, one launch (start us, length us, event | category | flops | bytes accessed | tf_op | source)
XLA Modules:
  0.0 37.8 jit_solution(17503015170041519158)
XLA Ops:
  0.0 37.0 %encoder_processor.1 = bf16[256,1024]{1,0:T(8,128)(2,1)S(1)} custom-call(s32[64]{0:T(128)} %count_s.1, s32[12,256]{1,0:T(8,128)} %enc_edges.1, bf16[4096,128]{1,0:T(8,128)(2,1)} %grid.1, bf16[256,1024]{1,0:T(8,128)(2,1)} %mesh_in.1, f32[96,256]{1,0:T(8,128)} %bitcast.3, f32[2056,256]{1,0:T(8,128)} %bitcast.2, bf16[128,1024]{1,0:T(8,128)(2,1)} %w_embed.1, ...), custom_call_target="tpu_custom_call" | custom-call | tf_op jit(solution)/shard_map/encoder_processor/pallas_call | solution.py:560
  37.0 0.8 %copy.20 = bf16[256,1024]{1,0:T(8,128)(2,1)} copy(bf16[256,1024]{1,0:T(8,128)(2,1)S(1)} %encoder_processor.1) | data formatting | bytes 1048576

commit v5 on v4

--- a/solution.py
+++ b/solution.py
@@ -36,11 +36,11 @@
 
 
 def kernel(
-    count_s, enc_edges, grid, mesh_in, enc_bias, proc_bias, w_embed,
+    counts, enc_edges, grid, mesh_in, enc_bias, proc_bias, w_embed,
     enc_query, enc_key, enc_value, enc_out,
     proc_query, proc_key, proc_value, proc_out, mlp_gate, mlp_up, mlp_down,
     out,
-    edge_s, ext, extf, mesh_v, we_v, eq_v, ek_v, ev_v, eo_v, pq_v, pk_v, pv_v, po_v,
+    count_s, edge_s, ext, extf, mesh_v, we_v, eq_v, ek_v, ev_v, eo_v, pq_v, pk_v, pv_v, po_v,
     gate_v, up_v, down_v, eb_v, pb_v, bd, qk, vmap, apart, marks, g, u_s, lat, nx, q_s, k_s, v_s,
     hid, part, peaks, sums, wo, psend, precv,
     load_sem, gs_sem, gr_sem, fs_sem, fr_sem, ds_sem, dr_sem, xs_sem, xr_sem, ls_sem, lr_sem,
@@ -78,6 +78,7 @@
     sources = [
         (mesh_in, mesh_v),
         (enc_edges.at[:, pl.ds(pl.multiple_of(core * half, LANES), half)], edge_s),
+        (counts, count_s),
         (enc_query, eq_v),
         (w_embed, we_v),
         (enc_key, ek_v),
@@ -101,12 +102,9 @@
         pltpu.make_async_copy(src, dst, load_sem.at[i]) for i, (src, dst) in enumerate(sources)
     ]
     (
-        l_mesh, l_edge, l_eq, l_we, l_ek, l_ev, l_eb0, l_eb1, l_pb0, l_pb1, l_grid, l_eo0, l_eo1,
+        l_mesh, l_edge, l_count, l_eq, l_we, l_ek, l_ev, l_eb0, l_eb1, l_pb0, l_pb1, l_grid, l_eo0, l_eo1,
         l_gate, l_up, l_pq, l_pk, l_pv, l_down, l_po,
     ) = loads
-    for load in loads[:10]:
-        load.start()
-
     barrier = pltpu.get_barrier_semaphore()
     def greet(device):
         pl.semaphore_signal(barrier, inc=1, device_id=device, device_id_type=pl.DeviceIdType.MESH)
@@ -119,6 +117,8 @@
 
     when(has_left, lambda: greet_band(left))
     when(has_right, lambda: greet_band(right))
+    for load in loads[:11]:
+        load.start()
     pl.semaphore_wait(barrier, 1 + jnp.where(has_left, 2, 0) + jnp.where(has_right, 2, 0))
 
     def remote(src, dst, send, recv, device):
@@ -174,9 +174,11 @@
         for copy in copies:
             copy.start()
 
-    when(has_right, lambda: start_all(halo[0::2] + direct[0::2]))
-    when(has_left, lambda: start_all(halo[1::2] + direct[1::2]))
-    for load in loads[10:]:
+    when(has_right, halo[0].start)
+    when(has_left, halo[1].start)
+    when(has_right, lambda: start_all(halo[2::2] + direct[0::2]))
+    when(has_left, lambda: start_all(halo[3::2] + direct[1::2]))
+    for load in loads[11:]:
         load.start()
 
     padding = eb_v.shape[1] - bias_rows
@@ -223,6 +225,7 @@
     reach = half
     span = nodes + 2 * reach
     window = 3 * half
+    l_count.wait()
     own_count = count_s[band]
     lower_count = jnp.where(has_left, count_s[left], 0)
     upper_count = jnp.where(has_right, count_s[right], 0)
@@ -308,10 +311,67 @@
                 g[pl.ds(block * block_rows + edge * BLOCK + n, 1), :] = found[n]
 
     ones = jnp.ones((block_rows, LANES), BF16)
-    gather(0)
-    for block in range(blocks):
-        if block + 1 < blocks:
-            gather(block + 1)
+    quarter = half // 2
+    eighth = quarter // 2
+    sixteenth = eighth // 2
+    parts = (
+        lambda which: pl.ds(pl.multiple_of(which * eighth, 16), eighth),
+        lambda which: pl.ds(pl.multiple_of(quarter + which * sixteenth, 16), sixteenth),
+        lambda which: pl.ds(quarter + eighth, eighth),
+    )
+
+    def window_copy(section, which, n):
+        rows = parts[section](which)
+        return remote(
+            nx.at[1 + core, rows], nx.at[3 * other, rows],
+            hs_sem.at[2 * section + n], hr_sem.at[3 * other + section], mesh_id(toward, which),
+        )
+
+    sends = [
+        window_copy(section, which, n) for section in range(3) for n, which in enumerate((core, other))
+    ]
+    to_sibling = [
+        remote(
+            lat.at[core, pl.ds(n * quarter, quarter)], lat.at[core, pl.ds(n * quarter, quarter)],
+            ls_sem.at[n], lr_sem.at[n], mesh_id(band, other),
+        )
+        for n in range(2)
+    ]
+    from_sibling = [
+        remote(
+            lat.at[other, pl.ds(n * quarter, quarter)], lat.at[other, pl.ds(n * quarter, quarter)],
+            ls_sem.at[n], lr_sem.at[n], mesh_id(band, other),
+        )
+        for n in range(2)
+    ]
+    handed = []
+    for d in range(2):
+        for section in range(2):
+            here = nx.at[3 * d, parts[section](core)]
+            handed.append(
+                remote(
+                    here, here, ks_sem.at[2 * d + section], kr_sem.at[2 * d + section],
+                    mesh_id(band, other),
+                )
+            )
+
+    def landed(d, section):
+        here = nx.at[3 * d, parts[section](core)]
+        remote(
+            here, here, hs_sem.at[2 * section], hr_sem.at[3 * d + section], mesh_id(toward, core)
+        ).wait_recv()
+
+    def hand(d):
+        for section in range(2):
+            landed(d, section)
+            handed[2 * d + section].start()
+
+    def all_here(d):
+        landed(d, 2)
+        for section in range(2):
+            handed[2 * d + section].wait_recv()
+
+    def attend(block):
         rows = slice(block * BLOCK, (block + 1) * BLOCK)
         near = g[block * block_rows : (block + 1) * block_rows, :].astype(BF16)
         asked = jnp.concatenate(
@@ -324,108 +384,74 @@
         mixed = (mixed[:, :LANES] / mixed[:, LANES:]).astype(BF16)
         for h in range(2 * local_heads):
             u_s[rows, h * LANES : (h + 1) * LANES] = mixed[h * BLOCK : (h + 1) * BLOCK]
-    attended = []
-    for pair in range(2 * pairs):
-        attended.append(nn(u_s[:, pair * 2 * LANES : (pair + 1) * 2 * LANES], vmap[pair]))
-    attended = jnp.concatenate(attended, 1).astype(BF16)
+
     l_eo0.wait()
     l_eo1.wait()
-    own_mesh = mesh_v[pl.ds(pl.multiple_of(core * half, half), half), :].astype(F32)
-    latent = (own_mesh + nn(attended, eo_v[...])).astype(BF16)
-    lat[core] = latent
-    to_sibling = remote(lat.at[core], lat.at[core], ls_sem.at[0], lr_sem.at[0], mesh_id(band, other))
-    to_sibling.start()
-    nx[1 + core] = normalize(latent.astype(F32))
-
-    third = half * 3 // 8
-    tail = pl.ds(2 * third, half - 2 * third)
-
-    def part_of(slot, which):
-        return nx.at[slot, pl.ds(pl.multiple_of(which * third, 16), third)]
-
-    sends = [
-        remote(
-            part_of(1 + core, which), part_of(3 * other, which),
-            hs_sem.at[i], hr_sem.at[2 * other], mesh_id(toward, which),
-        )
-        for i, which in enumerate((core, other))
-    ]
-    sends += [
-        remote(
-            nx.at[1 + core, tail], nx.at[3 * other, tail],
-            hs_sem.at[2 + i], hr_sem.at[2 * other + 1], mesh_id(toward, which),
-        )
-        for i, which in enumerate((core, other))
-    ]
-    when(has_toward, lambda: start_all(sends))
-    handed = [
-        remote(
-            part_of(s, core), part_of(s, core),
-            ks_sem.at[d], kr_sem.at[d], mesh_id(band, other),
-        )
-        for d, s in enumerate((0, 3))
-    ]
-
-    def hand(d):
-        s = 3 * d
-        remote(
-            part_of(s, core), part_of(s, core),
-            hs_sem.at[0], hr_sem.at[2 * d], mesh_id(toward, core),
-        ).wait_recv()
-        handed[d].start()
-
-    def all_here(d):
-        s = 3 * d
-        remote(
-            nx.at[s, tail], nx.at[s, tail],
-            hs_sem.at[2], hr_sem.at[2 * d + 1], mesh_id(toward, core),
-        ).wait_recv()
-        handed[d].wait_recv()
+    gather(0)
+    for n in range(2):
+        for block in range(n * blocks // 2, (n + 1) * blocks // 2):
+            if block + 1 < blocks:
+                gather(block + 1)
+            attend(block)
+        rows = slice(n * quarter, (n + 1) * quarter)
+        attended = jnp.concatenate(
+            [
+                nn(u_s[rows, pair * 2 * LANES : (pair + 1) * 2 * LANES], vmap[pair])
+                for pair in range(2 * pairs)
+            ],
+            1,
+        ).astype(BF16)
+        start = pl.multiple_of(core * half + n * quarter, quarter)
+        own_mesh = mesh_v[pl.ds(start, quarter), :].astype(F32)
+        latent = (own_mesh + nn(attended, eo_v[...])).astype(BF16)
+        lat[core, rows] = latent
+        to_sibling[n].start()
+        nx[1 + core, rows] = normalize(latent.astype(F32))
+        when(has_toward, lambda n=n: start_all(sends[:2] if n == 0 else sends[2:]))
 
     def clear(s):
         nx[s] = jnp.zeros((half, width), BF16)
 
     when(jnp.logical_not(has_left), lambda: clear(0))
     when(jnp.logical_not(has_right), lambda: clear(3))
-    to_sibling.wait_recv()
-    nx[2 - core] = normalize(lat[other].astype(F32))
-    normed = nx[1:3].reshape(nodes, width)
-
-    l_pq.wait()
-    win_query = nn(normed, pq_v[...]).astype(BF16)
-    win_query = win_query.astype(F32) * HDIM**-0.5
     first_head = iota((half, LANES), 1) < HDIM
-    for i in range(2):
-        for pair in range(pairs):
-            both = win_query[i * half : (i + 1) * half, pair * LANES : (pair + 1) * LANES]
-            q_s[i, pair, 0:half, :] = jnp.where(first_head, both, 0.0).astype(BF16)
-            q_s[i, pair, half:nodes, :] = jnp.where(first_head, 0.0, both).astype(BF16)
-    l_pk.wait()
-    l_pv.wait()
-
-    def keys_values(source, places):
-        keys = nn(source, pk_v[...]).astype(BF16)
-        values = nn(source, pv_v[...]).astype(BF16)
-        for n, rows in enumerate(places):
-            have = slice(n * half, (n + 1) * half)
-            k_s[rows, :] = keys[have]
-            for pair in range(pairs):
-                v_s[rows, pair * 2 * LANES : pair * 2 * LANES + LANES] = values[
-                    have, pair * LANES : (pair + 1) * LANES
-                ]
-
-    keys_values(normed, (slice(half, 2 * half), slice(2 * half, 3 * half)))
-    l_gate.wait()
-    l_up.wait()
     step = 512
     steps = gate_v.shape[1] // step
-    for ch in range(steps):
-        columns = slice(ch * step, (ch + 1) * step)
-        gated = nn(normed, gate_v[:, columns])
-        raised = nn(normed, up_v[:, columns])
-        hid[:, columns] = (0.5 * gated * (1.0 + jnp.tanh(0.5 * gated)) * raised).astype(BF16)
-    l_down.wait()
-    l_po.wait()
+
+    def keys_values(source, start):
+        rows = pl.ds(pl.multiple_of(start, half), half)
+        k_s[rows, :] = nn(source, pk_v[...]).astype(BF16)
+        values = nn(source, pv_v[...]).astype(BF16)
+        for pair in range(pairs):
+            v_s[rows, pair * 2 * LANES : pair * 2 * LANES + LANES] = values[
+                :, pair * LANES : (pair + 1) * LANES
+            ]
+
+    def project(which):
+        source = nx[1 + which]
+        win_query = nn(source, pq_v[...]).astype(BF16)
+        win_query = win_query.astype(F32) * HDIM**-0.5
+        for pair in range(pairs):
+            both = win_query[:, pair * LANES : (pair + 1) * LANES]
+            q_s[which, pair, 0:half, :] = jnp.where(first_head, both, 0.0).astype(BF16)
+            q_s[which, pair, half:nodes, :] = jnp.where(first_head, 0.0, both).astype(BF16)
+        keys_values(source, (1 + which) * half)
+        rows = pl.ds(pl.multiple_of(which * half, half), half)
+        for ch in range(steps):
+            columns = slice(ch * step, (ch + 1) * step)
+            gated = nn(source, gate_v[:, columns])
+            raised = nn(source, up_v[:, columns])
+            activated = 0.5 * gated * (1.0 + jnp.tanh(0.5 * gated)) * raised
+            hid[rows, columns] = activated.astype(BF16)
+
+    for load in (l_pq, l_pk, l_pv, l_gate, l_up, l_down, l_po):
+        load.wait()
+    project(core)
+    for copy in from_sibling:
+        copy.wait_recv()
+    nx[2 - core] = normalize(lat[other].astype(F32))
+    project(other)
+
     own_keys = slice(half, 3 * half)
     for i in (1, 0):
         held = slice((1 - i) * half, (3 - i) * half)
@@ -442,13 +468,13 @@
             sums[i, pair] = nn(weights, v_s[own_keys, pair * 2 * LANES : (pair + 1) * 2 * LANES])
     when(has_right, lambda: hand(1))
     when(has_left, lambda: hand(0))
-    results = [None, None]
+    results = [None] * 4
     for i in (1, 0):
         when(sides[i], lambda: all_here(i))
         rows = slice(i * half, (i + 1) * half)
         seen = slice(3 * i * half, (3 * i + 1) * half)
         held = slice(2 * i * half, (2 * i + 1) * half)
-        keys_values(nx[3 * i], (seen,))
+        keys_values(nx[3 * i], 3 * i * half)
         for pair in range(pairs):
             columns = slice(pair * LANES, (pair + 1) * LANES)
             scores = nt(q_s[i, pair], k_s[seen, columns]) + bd[pair, i, :, held]
@@ -461,27 +487,32 @@
             lower = sums[i, pair, :, LANES : 2 * LANES] * shrink + mixed[:, LANES:]
             mixed = upper / lower
             wo[rows, columns] = jnp.where(first_head, mixed[:half], mixed[half:]).astype(BF16)
-        psend[i] = (part[rows, :] + nn(wo[rows, :], po_v[...])).astype(BF16)
-        result = remote(
-            psend.at[i], precv.at[i], ps_sem.at[i], pr_sem.at[i], mesh_id(band, other)
-        )
-        result.start()
-        results[i] = result
+        for n in range(2):
+            columns = slice(n * width // 2, (n + 1) * width // 2)
+            psend[i, n] = (part[rows, columns] + nn(wo[rows, :], po_v[:, columns])).astype(BF16)
+            at = 2 * i + n
+            results[at] = remote(
+                psend.at[i, n], precv.at[i, n], ps_sem.at[at], pr_sem.at[at], mesh_id(band, other)
+            )
+            results[at].start()
     for i in (1, 0):
-        results[i].wait_recv()
-        summed = psend[i].astype(F32) + precv[i].astype(F32)
-        node = iota((half, width), 0) + i * half
+        node = iota((half, width // 2), 0) + i * half
         scale = (node < own_count).astype(F32)
-        out[i * half : (i + 1) * half, :] = ((lat[i].astype(F32) + summed) * scale).astype(BF16)
+        for n in range(2):
+            results[2 * i + n].wait_recv()
+            columns = slice(n * width // 2, (n + 1) * width // 2)
+            summed = psend[i, n].astype(F32) + precv[i, n].astype(F32)
+            total = lat[i, :, columns].astype(F32) + summed
+            out[i * half : (i + 1) * half, columns] = (total * scale).astype(BF16)
 
     def sent(copies):
         for copy in copies:
             copy.wait_send()
 
-    when(has_right, lambda: sent(halo[0::2] + direct[0::2] + passed[1::2] + handed[1:]))
-    when(has_left, lambda: sent(halo[1::2] + direct[1::2] + passed[0::2] + handed[:1]))
+    when(has_right, lambda: sent(halo[0::2] + direct[0::2] + passed[1::2] + handed[2:]))
+    when(has_left, lambda: sent(halo[1::2] + direct[1::2] + passed[0::2] + handed[:2]))
     when(has_toward, lambda: sent(sends))
-    sent([to_sibling] + results)
+    sent(to_sibling + results)
 
 
 def local(
@@ -498,10 +529,10 @@
     enc_bias = enc_bias.reshape(edges * heads, nodes)
     proc_bias = proc_bias.reshape(-1, nodes)
     anywhere = pl.BlockSpec(memory_space=pl.ANY)
-    in_scalar = pl.BlockSpec(memory_space=pltpu.SMEM)
     dma = pltpu.SemaphoreType.DMA
     vmem = pltpu.VMEM
     scratch = [
+        pltpu.SMEM(counts.shape, jnp.int32),
         pltpu.SMEM((edges, half), jnp.int32),
         vmem((RING * grid_rows, channels), BF16),
         vmem((RING * grid_rows, channels), F32),
@@ -537,9 +568,9 @@
         vmem((2, heads // 2, nodes, LANES), F32),
         vmem((2, heads // 2, nodes, 2 * LANES), F32),
         vmem((nodes, local_width), BF16),
-        vmem((2, half, width), BF16),
-        vmem((2, half, width), BF16),
-        dma((20,)),
+        vmem((2, 2, half, width // 2), BF16),
+        vmem((2, 2, half, width // 2), BF16),
+        dma((21,)),
         dma((2 * CHUNKS,)),
         dma((2 * CHUNKS,)),
         dma((2 * CHUNKS,)),
@@ -548,19 +579,19 @@
         dma((4,)),
         dma((2,)),
         dma((2,)),
-        dma((1,)),
-        dma((1,)),
+        dma((2,)),
+        dma((2,)),
+        dma((6,)),
+        dma((6,)),
         dma((4,)),
         dma((4,)),
-        dma((2,)),
-        dma((2,)),
-        dma((2,)),
-        dma((2,)),
+        dma((4,)),
+        dma((4,)),
     ]
     return pl.pallas_call(
         kernel,
         out_shape=pltpu.VMEM((nodes, width), BF16),
-        in_specs=[in_scalar] + [anywhere] * 17,
+        in_specs=[anywhere] * 18,
         out_specs=pl.BlockSpec(memory_space=pltpu.VMEM),
         scratch_shapes=scratch,
         compiler_params=pltpu.CompilerParams(

time: 37.9 us -> 37.2 us (0.982)
  Pallas kernels: 37 us -> 36.3 us
    pallas_call x1, Pallas kernels: 37 us -> 36.3 us  [local(): pl.pallas_call(kernel, out_shape=pltpu.VMEM((nodes, width), BF16), in_spe...]
where the time goes in v5:
time: 37.2 us; the launch traced here: 37.1 us
  Pallas kernels  36.3 us (98%)
  local copies, waits for them, and re-layouts  0.8 us (2%)
    pallas_call x1, Pallas kernels, local(): pl.pallas_call(kernel, out_shape=pltpu.VMEM((nodes, width), BF16), in_spe...  36.3 us
    unnamed x1, local copies, waits for them, and re-layouts  0.8 us

profile of v5, /device:TPU:97, one launch (start us, length us, event | category | flops | bytes accessed | tf_op | source)
XLA Modules:
  0.0 37.1 jit_solution(15072680942812960197)
XLA Ops:
  0.0 36.3 %encoder_processor.1 = bf16[256,1024]{1,0:T(8,128)(2,1)S(1)} custom-call(s32[64]{0:T(128)} %counts.1, s32[12,256]{1,0:T(8,128)} %enc_edges.1, bf16[4096,128]{1,0:T(8,128)(2,1)} %grid.1, bf16[256,1024]{1,0:T(8,128)(2,1)} %mesh_in.1, f32[96,256]{1,0:T(8,128)} %bitcast.3, f32[2056,256]{1,0:T(8,128)} %bitcast.2, bf16[128,1024]{1,0:T(8,128)(2,1)} %w_embed.1, ...), custom_call_target="tpu_custom_call" | custom-call | tf_op jit(solution)/shard_map/encoder_processor/pallas_call | solution.py:591
  36.3 0.8 %copy.20 = bf16[256,1024]{1,0:T(8,128)(2,1)} copy(bf16[256,1024]{1,0:T(8,128)(2,1)S(1)} %encoder_processor.1) | data formatting | bytes 1048576

commit v6 on v5

--- a/solution.py
+++ b/solution.py
@@ -12,7 +12,8 @@
 BF16 = jnp.bfloat16
 LANES = 128
 BLOCK = 16
-CHUNKS = 8
+SHARES = (4, 4, 4, 3)
+CHUNKS = len(SHARES)
 RING = 4
 VMEM_BYTES = 60 * 1024 * 1024
 
@@ -23,6 +24,11 @@
 
 def nt(left, right):
     return lax.dot_general(left, right, (((1,), (1,)), ((), ())), preferred_element_type=F32)
+
+
+def inverse(values):
+    guess = pl.reciprocal(values, approx=True)
+    return guess * (2.0 - values * guess)
 
 
 def iota(shape, dim):
@@ -76,6 +82,7 @@
     theirs = pl.ds(pl.multiple_of(other * local_width, LANES), local_width)
     bias_rows = enc_bias.shape[0]
     sources = [
+        (grid, ext.at[ring_rows(band, 0, grid_rows)]),
         (mesh_in, mesh_v),
         (enc_edges.at[:, pl.ds(pl.multiple_of(core * half, LANES), half)], edge_s),
         (counts, count_s),
@@ -87,7 +94,6 @@
         (enc_bias.at[:, pl.ds(half, half)], eb_v.at[1, pl.ds(0, bias_rows)]),
         (proc_bias.at[:, pl.ds(0, half)], pb_v.at[0]),
         (proc_bias.at[:, pl.ds(half, half)], pb_v.at[1]),
-        (grid, ext.at[ring_rows(band, 0, grid_rows)]),
         (enc_out.at[own], eo_v.at[pl.ds(0, local_width)]),
         (enc_out.at[theirs], eo_v.at[pl.ds(local_width, local_width)]),
         (mlp_gate, gate_v),
@@ -102,22 +108,21 @@
         pltpu.make_async_copy(src, dst, load_sem.at[i]) for i, (src, dst) in enumerate(sources)
     ]
     (
-        l_mesh, l_edge, l_count, l_eq, l_we, l_ek, l_ev, l_eb0, l_eb1, l_pb0, l_pb1, l_grid, l_eo0, l_eo1,
+        l_grid, l_mesh, l_edge, l_count, l_eq, l_we, l_ek, l_ev, l_eb0, l_eb1, l_pb0, l_pb1, l_eo0, l_eo1,
         l_gate, l_up, l_pq, l_pk, l_pv, l_down, l_po,
     ) = loads
     barrier = pltpu.get_barrier_semaphore()
     def greet(device):
         pl.semaphore_signal(barrier, inc=1, device_id=device, device_id_type=pl.DeviceIdType.MESH)
 
-    greet(mesh_id(band, other))
-
     def greet_band(b):
         greet(mesh_id(b, core))
         greet(mesh_id(b, other))
 
+    when(has_right, lambda: greet_band(right))
     when(has_left, lambda: greet_band(left))
-    when(has_right, lambda: greet_band(right))
-    for load in loads[:11]:
+    greet(mesh_id(band, other))
+    for load in loads[:8]:
         load.start()
     pl.semaphore_wait(barrier, 1 + jnp.where(has_left, 2, 0) + jnp.where(has_right, 2, 0))
 
@@ -127,20 +132,21 @@
             device_id=device, device_id_type=pl.DeviceIdType.MESH,
         )
 
-    piece = grid_rows // 2 // CHUNKS
-    last_piece = piece // 2
-    sizes = [piece] * (CHUNKS - 1) + [piece - last_piece]
+    unit = grid_rows // 2 // 16
+    sizes = [share * unit for share in SHARES]
+    starts = [sum(sizes[:k]) for k in range(CHUNKS)]
+    last_piece = grid_rows // 2 - sum(sizes)
     halo = []
     passed = []
     direct = []
     landing = []
     for k, size in enumerate(sizes):
-        start = core * (grid_rows // 2) + k * piece
+        start = core * (grid_rows // 2) + starts[k]
         for d, (target, source) in enumerate(((right, left), (left, right))):
             slot = d * CHUNKS + k
             halo.append(
                 remote(
-                    grid.at[pl.ds(pl.multiple_of(start, LANES), size)],
+                    ext.at[ring_rows(band, start, size)],
                     ext.at[ring_rows(band, start, size)],
                     gs_sem.at[slot], gr_sem.at[slot], mesh_id(target, core),
                 )
@@ -155,10 +161,10 @@
 
     for n, peer in enumerate((core, other)):
         for d, (target, source) in enumerate(((right, left), (left, right))):
-            mine = pl.ds(pl.multiple_of(direct_start(core), LANES), last_piece)
+            mine = ring_rows(band, direct_start(core), last_piece)
             direct.append(
                 remote(
-                    grid.at[mine], ext.at[ring_rows(band, direct_start(core), last_piece)],
+                    ext.at[mine], ext.at[mine],
                     ds_sem.at[2 * n + d], dr_sem.at[2 * n + d], mesh_id(target, peer),
                 )
             )
@@ -174,11 +180,12 @@
         for copy in copies:
             copy.start()
 
+    l_grid.wait()
+    when(has_left, halo[1].start)
     when(has_right, halo[0].start)
-    when(has_left, halo[1].start)
+    when(has_left, lambda: start_all(halo[3::2] + direct[1::2]))
     when(has_right, lambda: start_all(halo[2::2] + direct[0::2]))
-    when(has_left, lambda: start_all(halo[3::2] + direct[1::2]))
-    for load in loads[11:]:
+    for load in loads[8:]:
         load.start()
 
     padding = eb_v.shape[1] - bias_rows
@@ -258,11 +265,11 @@
     def arrive(k, d):
         halo[2 * k + d].wait_recv()
         passed[2 * k + d].start()
-        widen(ring_rows((left, right)[d], core * (grid_rows // 2) + k * piece, sizes[k]))
+        widen(ring_rows((left, right)[d], core * (grid_rows // 2) + starts[k], sizes[k]))
 
     def arrive_passed(k, d):
         passed[2 * k + d].wait_recv()
-        widen(ring_rows((left, right)[d], other * (grid_rows // 2) + k * piece, sizes[k]))
+        widen(ring_rows((left, right)[d], other * (grid_rows // 2) + starts[k], sizes[k]))
 
     def arrive_direct(d):
         for n, peer in enumerate((core, other)):
@@ -284,16 +291,16 @@
         unused = slice(block * block_rows + edges * BLOCK, (block + 1) * block_rows)
         g[unused, :] = jnp.zeros((block_rows - edges * BLOCK, LANES), F32)
     l_edge.wait()
-    l_grid.wait()
     for h in range(local_heads):
         window_bias(h)
     for k in range(CHUNKS):
-        widen(ring_rows(band, 2 * k * piece, 2 * piece))
+        widen(ring_rows(band, 2 * starts[k], 2 * sizes[k]))
         for d in range(2):
             when(sides[d], lambda k=k, d=d: arrive(k, d))
         if k > 0:
             for d in range(2):
                 when(sides[d], lambda k=k, d=d: arrive_passed(k - 1, d))
+    widen(ring_rows(band, grid_rows - 2 * last_piece, 2 * last_piece))
     for copy in exchange:
         copy.wait()
     for d in range(2):
@@ -381,33 +388,30 @@
         peak = jnp.max(scores, 1, keepdims=True)
         weights = jnp.exp(scores - peak).astype(BF16)
         mixed = nn(weights, jnp.concatenate([near, ones], 1))
-        mixed = (mixed[:, :LANES] / mixed[:, LANES:]).astype(BF16)
+        mixed = (mixed[:, :LANES] * inverse(mixed[:, LANES:])).astype(BF16)
         for h in range(2 * local_heads):
             u_s[rows, h * LANES : (h + 1) * LANES] = mixed[h * BLOCK : (h + 1) * BLOCK]
 
     l_eo0.wait()
     l_eo1.wait()
     gather(0)
-    for n in range(2):
-        for block in range(n * blocks // 2, (n + 1) * blocks // 2):
-            if block + 1 < blocks:
-                gather(block + 1)
-            attend(block)
-        rows = slice(n * quarter, (n + 1) * quarter)
-        attended = jnp.concatenate(
-            [
-                nn(u_s[rows, pair * 2 * LANES : (pair + 1) * 2 * LANES], vmap[pair])
-                for pair in range(2 * pairs)
-            ],
-            1,
-        ).astype(BF16)
-        start = pl.multiple_of(core * half + n * quarter, quarter)
-        own_mesh = mesh_v[pl.ds(start, quarter), :].astype(F32)
-        latent = (own_mesh + nn(attended, eo_v[...])).astype(BF16)
-        lat[core, rows] = latent
-        to_sibling[n].start()
-        nx[1 + core, rows] = normalize(latent.astype(F32))
-        when(has_toward, lambda n=n: start_all(sends[:2] if n == 0 else sends[2:]))
+    for block in range(blocks):
+        if block + 1 < blocks:
+            gather(block + 1)
+        attend(block)
+    attended = jnp.concatenate(
+        [
+            nn(u_s[:, pair * 2 * LANES : (pair + 1) * 2 * LANES], vmap[pair])
+            for pair in range(2 * pairs)
+        ],
+        1,
+    ).astype(BF16)
+    own_mesh = mesh_v[pl.ds(pl.multiple_of(core * half, half), half), :].astype(F32)
+    latent = (own_mesh + nn(attended, eo_v[...])).astype(BF16)
+    lat[core] = latent
+    nx[1 + core] = normalize(latent.astype(F32))
+    when(has_toward, lambda: start_all(sends))
+    start_all(to_sibling)
 
     def clear(s):
         nx[s] = jnp.zeros((half, width), BF16)
@@ -452,6 +456,7 @@
     nx[2 - core] = normalize(lat[other].astype(F32))
     project(other)
 
+    when(has_right, lambda: hand(1))
     own_keys = slice(half, 3 * half)
     for i in (1, 0):
         held = slice((1 - i) * half, (3 - i) * half)
@@ -466,7 +471,6 @@
             weights = jnp.exp(scores - peak).astype(BF16)
             peaks[i, pair] = jnp.broadcast_to(peak, (nodes, LANES))
             sums[i, pair] = nn(weights, v_s[own_keys, pair * 2 * LANES : (pair + 1) * 2 * LANES])
-    when(has_right, lambda: hand(1))
     when(has_left, lambda: hand(0))
     results = [None] * 4
     for i in (1, 0):
@@ -485,7 +489,7 @@
             shrink = jnp.exp(before - peak)
             upper = sums[i, pair, :, 0:LANES] * shrink + mixed[:, :LANES]
             lower = sums[i, pair, :, LANES : 2 * LANES] * shrink + mixed[:, LANES:]
-            mixed = upper / lower
+            mixed = upper * inverse(lower)
             wo[rows, columns] = jnp.where(first_head, mixed[:half], mixed[half:]).astype(BF16)
         for n in range(2):
             columns = slice(n * width // 2, (n + 1) * width // 2)

time: 37.2 us -> 36.7 us (0.987)
  Pallas kernels: 36.3 us -> 35.8 us
    pallas_call x1, Pallas kernels: 36.3 us -> 35.8 us  [local(): pl.pallas_call(kernel, out_shape=pltpu.VMEM((nodes, width), BF16), in_spe...]
where the time goes in v6:
time: 36.7 us; the launch traced here: 36.6 us
  Pallas kernels  35.8 us (98%)
  local copies, waits for them, and re-layouts  0.8 us (2%)
    pallas_call x1, Pallas kernels, local(): pl.pallas_call(kernel, out_shape=pltpu.VMEM((nodes, width), BF16), in_spe...  35.8 us
    unnamed x1, local copies, waits for them, and re-layouts  0.8 us

profile of v6, /device:TPU:97, one launch (start us, length us, event | category | flops | bytes accessed | tf_op | source)
XLA Modules:
  0.0 36.6 jit_solution(14369608092027915138)
XLA Ops:
  0.0 35.8 %encoder_processor.1 = bf16[256,1024]{1,0:T(8,128)(2,1)S(1)} custom-call(s32[64]{0:T(128)} %counts.1, s32[12,256]{1,0:T(8,128)} %enc_edges.1, bf16[4096,128]{1,0:T(8,128)(2,1)} %grid.1, bf16[256,1024]{1,0:T(8,128)(2,1)} %mesh_in.1, f32[96,256]{1,0:T(8,128)} %bitcast.3, f32[2056,256]{1,0:T(8,128)} %bitcast.2, bf16[128,1024]{1,0:T(8,128)(2,1)} %w_embed.1, ...), custom_call_target="tpu_custom_call" | custom-call | tf_op jit(solution)/shard_map/encoder_processor/pallas_call | solution.py:595
  35.8 0.8 %copy.20 = bf16[256,1024]{1,0:T(8,128)(2,1)} copy(bf16[256,1024]{1,0:T(8,128)(2,1)S(1)} %encoder_processor.1) | data formatting | bytes 1048576

commit v7 on v6

--- a/solution.py
+++ b/solution.py
@@ -12,7 +12,7 @@
 BF16 = jnp.bfloat16
 LANES = 128
 BLOCK = 16
-SHARES = (4, 4, 4, 3)
+SHARES = (4, 4, 4, 3, 1)
 CHUNKS = len(SHARES)
 RING = 4
 VMEM_BYTES = 60 * 1024 * 1024
@@ -49,7 +49,7 @@
     count_s, edge_s, ext, extf, mesh_v, we_v, eq_v, ek_v, ev_v, eo_v, pq_v, pk_v, pv_v, po_v,
     gate_v, up_v, down_v, eb_v, pb_v, bd, qk, vmap, apart, marks, g, u_s, lat, nx, q_s, k_s, v_s,
     hid, part, peaks, sums, wo, psend, precv,
-    load_sem, gs_sem, gr_sem, fs_sem, fr_sem, ds_sem, dr_sem, xs_sem, xr_sem, ls_sem, lr_sem,
+    load_sem, gs_sem, gr_sem, fs_sem, fr_sem, xs_sem, xr_sem, ls_sem, lr_sem,
     hs_sem, hr_sem, ks_sem, kr_sem, ps_sem, pr_sem,
 ):
     band, core = lax.axis_index("band"), lax.axis_index("head")
@@ -59,6 +59,8 @@
     left, right = jnp.maximum(band - 1, 0), jnp.minimum(band + 1, bands - 1)
     toward = jnp.where(core == 1, right, left)
     has_toward = band != toward
+    beyond = jnp.where(core == 1, left, right)
+    has_beyond = band != beyond
     grid_rows = grid.shape[0]
     nodes = mesh_in.shape[0]
     half = nodes // 2
@@ -135,44 +137,32 @@
     unit = grid_rows // 2 // 16
     sizes = [share * unit for share in SHARES]
     starts = [sum(sizes[:k]) for k in range(CHUNKS)]
-    last_piece = grid_rows // 2 - sum(sizes)
-    halo = []
-    passed = []
-    direct = []
-    landing = []
-    for k, size in enumerate(sizes):
-        start = core * (grid_rows // 2) + starts[k]
-        for d, (target, source) in enumerate(((right, left), (left, right))):
-            slot = d * CHUNKS + k
-            halo.append(
+
+    def piece_of(b, which, k):
+        return ext.at[ring_rows(b, which * (grid_rows // 2) + starts[k], sizes[k])]
+
+    to_right, to_left, halo, passed, passing = [], [], [], [], []
+    for k in range(CHUNKS):
+        mine = piece_of(band, core, k)
+        for d, (copies, device) in enumerate(
+            ((to_right, mesh_id(right, 0)), (to_left, mesh_id(left, 1)))
+        ):
+            copies.append(
                 remote(
-                    ext.at[ring_rows(band, start, size)],
-                    ext.at[ring_rows(band, start, size)],
-                    gs_sem.at[slot], gr_sem.at[slot], mesh_id(target, core),
+                    mine, mine, gs_sem.at[d * CHUNKS + k], gr_sem.at[core * CHUNKS + k], device
                 )
             )
-            here = ext.at[ring_rows(source, start, size)]
+        for which in range(2):
+            slot = which * CHUNKS + k
+            near, far = piece_of(toward, which, k), piece_of(beyond, which, k)
+            halo.append(
+                remote(near, near, gs_sem.at[slot], gr_sem.at[slot], mesh_id(toward, other))
+            )
+            passing.append(
+                remote(near, near, fs_sem.at[slot], fr_sem.at[slot], mesh_id(band, other))
+            )
             passed.append(
-                remote(here, here, fs_sem.at[slot], fr_sem.at[slot], mesh_id(band, other))
-            )
-
-    def direct_start(which):
-        return which * (grid_rows // 2) + grid_rows // 2 - last_piece
-
-    for n, peer in enumerate((core, other)):
-        for d, (target, source) in enumerate(((right, left), (left, right))):
-            mine = ring_rows(band, direct_start(core), last_piece)
-            direct.append(
-                remote(
-                    ext.at[mine], ext.at[mine],
-                    ds_sem.at[2 * n + d], dr_sem.at[2 * n + d], mesh_id(target, peer),
-                )
-            )
-            here = ext.at[ring_rows(source, direct_start(peer), last_piece)]
-            landing.append(
-                remote(
-                    here, here, ds_sem.at[2 * n + d], dr_sem.at[2 * n + d], mesh_id(target, peer)
-                )
+                remote(far, far, fs_sem.at[slot], fr_sem.at[slot], mesh_id(band, other))
             )
     sides = (has_left, has_right)
 
@@ -181,10 +171,10 @@
             copy.start()
 
     l_grid.wait()
-    when(has_left, halo[1].start)
-    when(has_right, halo[0].start)
-    when(has_left, lambda: start_all(halo[3::2] + direct[1::2]))
-    when(has_right, lambda: start_all(halo[2::2] + direct[0::2]))
+    when(has_left, to_left[0].start)
+    when(has_right, to_right[0].start)
+    when(has_left, lambda: start_all(to_left[1:]))
+    when(has_right, lambda: start_all(to_right[1:]))
     for load in loads[8:]:
         load.start()
 
@@ -262,19 +252,17 @@
     def widen(rows):
         extf[rows, :] = ext[rows, :].astype(F32)
 
-    def arrive(k, d):
-        halo[2 * k + d].wait_recv()
-        passed[2 * k + d].start()
-        widen(ring_rows((left, right)[d], core * (grid_rows // 2) + starts[k], sizes[k]))
-
-    def arrive_passed(k, d):
-        passed[2 * k + d].wait_recv()
-        widen(ring_rows((left, right)[d], other * (grid_rows // 2) + starts[k], sizes[k]))
-
-    def arrive_direct(d):
-        for n, peer in enumerate((core, other)):
-            landing[2 * n + d].wait_recv()
-            widen(ring_rows((left, right)[d], direct_start(peer), last_piece))
+    def arrive(k):
+        for which in range(2):
+            halo[2 * k + which].wait_recv()
+            passing[2 * k + which].start()
+        for which in range(2):
+            widen(ring_rows(toward, which * (grid_rows // 2) + starts[k], sizes[k]))
+
+    def arrive_passed(k):
+        for which in range(2):
+            passed[2 * k + which].wait_recv()
+            widen(ring_rows(beyond, which * (grid_rows // 2) + starts[k], sizes[k]))
 
     blocks = half // BLOCK
     block_rows = 16 * BLOCK
@@ -295,18 +283,12 @@
         window_bias(h)
     for k in range(CHUNKS):
         widen(ring_rows(band, 2 * starts[k], 2 * sizes[k]))
-        for d in range(2):
-            when(sides[d], lambda k=k, d=d: arrive(k, d))
+        when(has_toward, lambda k=k: arrive(k))
         if k > 0:
-            for d in range(2):
-                when(sides[d], lambda k=k, d=d: arrive_passed(k - 1, d))
-    widen(ring_rows(band, grid_rows - 2 * last_piece, 2 * last_piece))
+            when(has_beyond, lambda k=k: arrive_passed(k - 1))
     for copy in exchange:
         copy.wait()
-    for d in range(2):
-        when(sides[d], lambda d=d: arrive_direct(d))
-    for d in range(2):
-        when(sides[d], lambda d=d: arrive_passed(CHUNKS - 1, d))
+    when(has_beyond, lambda: arrive_passed(CHUNKS - 1))
 
     def gather(block):
         for edge in range(edges):
@@ -513,9 +495,9 @@
         for copy in copies:
             copy.wait_send()
 
-    when(has_right, lambda: sent(halo[0::2] + direct[0::2] + passed[1::2] + handed[2:]))
-    when(has_left, lambda: sent(halo[1::2] + direct[1::2] + passed[0::2] + handed[:2]))
-    when(has_toward, lambda: sent(sends))
+    when(has_right, lambda: sent(to_right + handed[2:]))
+    when(has_left, lambda: sent(to_left + handed[:2]))
+    when(has_toward, lambda: sent(sends + passing))
     sent(to_sibling + results)
 
 
@@ -579,8 +561,6 @@
         dma((2 * CHUNKS,)),
         dma((2 * CHUNKS,)),
         dma((2 * CHUNKS,)),
-        dma((4,)),
-        dma((4,)),
         dma((2,)),
         dma((2,)),
         dma((2,)),

time: 36.7 us -> 35.5 us (0.967)
  Pallas kernels: 35.8 us -> 34.6 us
    pallas_call x1, Pallas kernels: 35.8 us -> 34.6 us  [local(): pl.pallas_call(kernel, out_shape=pltpu.VMEM((nodes, width), BF16), in_spe...]
where the time goes in v7:
time: 35.5 us; the launch traced here: 35.4 us
  Pallas kernels  34.6 us (97%)
  local copies, waits for them, and re-layouts  0.8 us (2%)
    pallas_call x1, Pallas kernels, local(): pl.pallas_call(kernel, out_shape=pltpu.VMEM((nodes, width), BF16), in_spe...  34.6 us
    unnamed x1, local copies, waits for them, and re-layouts  0.8 us

profile of v7, /device:TPU:97, one launch (start us, length us, event | category | flops | bytes accessed | tf_op | source)
XLA Modules:
  0.0 35.4 jit_solution(16055977033880383030)
XLA Ops:
  0.0 34.6 %encoder_processor.1 = bf16[256,1024]{1,0:T(8,128)(2,1)S(1)} custom-call(s32[64]{0:T(128)} %counts.1, s32[12,256]{1,0:T(8,128)} %enc_edges.1, bf16[4096,128]{1,0:T(8,128)(2,1)} %grid.1, bf16[256,1024]{1,0:T(8,128)(2,1)} %mesh_in.1, f32[96,256]{1,0:T(8,128)} %bitcast.3, f32[2056,256]{1,0:T(8,128)} %bitcast.2, bf16[128,1024]{1,0:T(8,128)(2,1)} %w_embed.1, ...), custom_call_target="tpu_custom_call" | custom-call | tf_op jit(solution)/shard_map/encoder_processor/pallas_call | solution.py:575
  34.6 0.8 %copy.20 = bf16[256,1024]{1,0:T(8,128)(2,1)} copy(bf16[256,1024]{1,0:T(8,128)(2,1)S(1)} %encoder_processor.1) | data formatting | bytes 1048576

commit v8 on v7

--- a/solution.py
+++ b/solution.py
@@ -438,9 +438,10 @@
     nx[2 - core] = normalize(lat[other].astype(F32))
     project(other)
 
-    when(has_right, lambda: hand(1))
     own_keys = slice(half, 3 * half)
     for i in (1, 0):
+        if i == 0:
+            when(has_right, lambda: hand(1))
         held = slice((1 - i) * half, (3 - i) * half)
         for pair in range(pairs):
             if pair % 2 == 0:

time: 35.5 us -> 35.5 us (level)
  no operation moved by 1% of the time
where the time goes in v8:
time: 35.5 us; the launch traced here: 35.4 us
  Pallas kernels  34.6 us (97%)
  local copies, waits for them, and re-layouts  0.8 us (2%)
    pallas_call x1, Pallas kernels, local(): pl.pallas_call(kernel, out_shape=pltpu.VMEM((nodes, width), BF16), in_spe...  34.6 us
    unnamed x1, local copies, waits for them, and re-layouts  0.8 us

profile of v8, /device:TPU:97, one launch (start us, length us, event | category | flops | bytes accessed | tf_op | source)
XLA Modules:
  0.0 35.4 jit_solution(17547565291909638896)
XLA Ops:
  0.0 34.6 %encoder_processor.1 = bf16[256,1024]{1,0:T(8,128)(2,1)S(1)} custom-call(s32[64]{0:T(128)} %counts.1, s32[12,256]{1,0:T(8,128)} %enc_edges.1, bf16[4096,128]{1,0:T(8,128)(2,1)} %grid.1, bf16[256,1024]{1,0:T(8,128)(2,1)} %mesh_in.1, f32[96,256]{1,0:T(8,128)} %bitcast.3, f32[2056,256]{1,0:T(8,128)} %bitcast.2, bf16[128,1024]{1,0:T(8,128)(2,1)} %w_embed.1, ...), custom_call_target="tpu_custom_call" | custom-call | tf_op jit(solution)/shard_map/encoder_processor/pallas_call | solution.py:576
  34.6 0.8 %copy.20 = bf16[256,1024]{1,0:T(8,128)(2,1)} copy(bf16[256,1024]{1,0:T(8,128)(2,1)S(1)} %encoder_processor.1) | data formatting | bytes 1048576
